TPU v7x, 512 devices: a whole 4x4x16 slice. The times are simulated.
512 devices in a mesh: bank: 256 (over x, y, z), det: 2 (over core).
Axes of the slice: x: 4, y: 4, z: 16, core: 2. Of those that a mesh axis runs over, the one named last changes fastest.
Arguments:
- strain: float32 [2, 2, 65536], P('det', None, 'bank'), may hold values from -6 to 6
- asd_inv: float32 [2, 65536], P('det', 'bank'), may hold values from 0.5 to 2
- indices: int32 [4096], P('bank'), may hold values from 0 to 16383
- counts: int32 [256], P('bank'), may hold values from 1 to 16, as said below
- sky_delay: int32 [16], replicated, may hold values from -21 to 21, as said below
- gain_near: float32 [16], replicated, may hold values from 0.2 to 1
- gain_far: float32 [16], replicated, may hold values from -1 to 1
Outputs:
- coherent: float32 [4096, 16, 4096], P('bank', None, 'det')
Inputs may be any that keep to these rules, and one draw needn't show every extreme that they name: `counts`: filled slots of each bank index; some bank index fills all 16. `sky_delay`: both extreme delays occur.
All inputs are finite; a program needn't handle non-finite values.
Results may differ from a plain program's by a relative error of at most 0.01.
Values may be sent and summed in bfloat16 or wider, within the bound.
No kernel may reach another device: no remote copies, remote signals or barrier semaphores. Data moves between devices by JAX's collectives and lax.ppermute only.
A program may use at most 64 MiB of HBM per device.

v0:
```python
import math

import jax
import jax.numpy as jnp
from jax import lax
from jax.sharding import PartitionSpec as P

DFT_ROWS = 512
DFT_COLS = 256
SAMPLES = 131072
BINS = 65536
LOW_BIN = 1920
WIN_BLOCKS = 8
WINDOW = 4096
SERIES = 5120


MSUN_SEC = 4.925491e-06
SAMPLE_RATE = 2048.0


def template_terms(table_index):
    total_mass = 6.0 * jnp.power(1.03, (table_index % 64).astype(jnp.float32))
    sym_ratio = 0.16 + 0.09 * (table_index // 64 % 64).astype(jnp.float32) / 63.0
    spin_value = -0.6 + 0.4 * (table_index // 4096).astype(jnp.float32)
    seconds = total_mass * MSUN_SEC
    return (seconds, sym_ratio, spin_value * (113.0 - 76.0 * sym_ratio) / 12.0)


def amplitude(seconds, frequency):
    clipped = jnp.maximum(frequency, 1.0)
    cutoff = 1.0 / (6.0**1.5 * math.pi * seconds)
    scaled = clipped / cutoff
    return clipped ** (-7.0 / 6.0) * jnp.exp(-(scaled * scaled) * (scaled * scaled))


def phase(seconds, sym_ratio, orbit_term, frequency):
    clipped = jnp.maximum(frequency, 1.0)
    velocity = (math.pi * seconds * clipped) ** (1.0 / 3.0)
    square = velocity * velocity
    leading = 3.0 / (128.0 * sym_ratio * square * square * velocity)
    series_terms = (
        1.0
        + (3715.0 / 756.0 + 55.0 * sym_ratio / 9.0) * square
        + (4.0 * orbit_term - 16.0 * math.pi) * square * velocity
    )
    return leading * series_terms - math.pi / 4.0


def transform_tables():
    rows_t = jnp.arange(DFT_ROWS)[:, None]
    cols_k = jnp.arange(DFT_ROWS // 2)[None, :]
    angle_one = 2.0 * math.pi / DFT_ROWS * (rows_t * cols_k % DFT_ROWS).astype(jnp.float32)
    cosine_one = jnp.cos(angle_one).astype(jnp.bfloat16)
    sine_one = jnp.sin(angle_one).astype(jnp.bfloat16)
    first_table = jnp.concatenate(
        [jnp.concatenate([cosine_one, -sine_one], 1), jnp.concatenate([sine_one, cosine_one], 1)], 0
    )
    twist_bins = jnp.arange(DFT_COLS)[None, :]
    angle_two = 2.0 * math.pi / SAMPLES * (rows_t * twist_bins % SAMPLES).astype(jnp.float32)
    twist_cos = jnp.cos(angle_two)
    twist_sin = jnp.sin(angle_two)
    inner_k = jnp.arange(DFT_COLS)[:, None]
    column_t = DFT_COLS // 2 - WIN_BLOCKS // 2 - 1 + jnp.arange(WIN_BLOCKS + 2)[None, :]
    angle_three = 2.0 * math.pi / DFT_COLS * (inner_k * column_t % DFT_COLS).astype(jnp.float32)
    cosine_three = jnp.cos(angle_three).astype(jnp.bfloat16)
    sine_three = jnp.sin(angle_three).astype(jnp.bfloat16)
    last_table = jnp.concatenate(
        [
            jnp.concatenate([cosine_three, sine_three], 1),
            jnp.concatenate([-sine_three, cosine_three], 1),
        ],
        0,
    )
    return (first_table, twist_cos, twist_sin, last_table)


def filter_template(over_white, envelope, phase_angle, tables):
    first_table, twist_cos, twist_sin, last_table = tables
    cosine = envelope * jnp.cos(phase_angle)
    sine = envelope * jnp.sin(phase_angle)
    real_part = over_white[0] * cosine - over_white[1] * sine
    imag_part = over_white[0] * sine + over_white[1] * cosine
    stacked = jnp.concatenate(
        [real_part.reshape(DFT_ROWS // 2, DFT_COLS), imag_part.reshape(DFT_ROWS // 2, DFT_COLS)], 0
    ).astype(jnp.bfloat16)
    middle = jnp.dot(first_table, stacked, preferred_element_type=jnp.float32)
    upper = middle[:DFT_ROWS]
    lower = middle[DFT_ROWS:]
    twisted = jnp.concatenate(
        [upper * twist_cos - lower * twist_sin, upper * twist_sin + lower * twist_cos], 1
    ).astype(jnp.bfloat16)
    result = jnp.dot(twisted, last_table, preferred_element_type=jnp.float32)
    width = WIN_BLOCKS + 2
    return jnp.stack([result[:, :width].T.reshape(-1), result[:, width:].T.reshape(-1)])


def coherent_stat(first_win, second_win, offset, length, delays, gain_near, gain_far):
    near_part = first_win[..., offset : offset + length].astype(jnp.float32)

    def per_sky(lag_samples, weight_near, weight_far):
        far_part = lax.dynamic_slice_in_dim(
            second_win, offset + lag_samples, length, second_win.ndim - 1
        ).astype(jnp.float32)
        real_part = weight_near * near_part[..., 0, :] + weight_far * far_part[..., 0, :]
        imag_part = weight_near * near_part[..., 1, :] + weight_far * far_part[..., 1, :]
        return (real_part * real_part + imag_part * imag_part) / (
            weight_near * weight_near + weight_far * weight_far
        )

    return jax.vmap(per_sky, in_axes=(0, 0, 0), out_axes=-2)(delays, gain_near, gain_far)


def on_device(strain, asd_inv, indices, counts, sky_delay, gain_near, gain_far):
    weight_sq = asd_inv[0] * asd_inv[0]
    over_local = strain[0] * weight_sq[None, :]
    tpl_slots = indices.shape[0]
    bin_ids = jnp.arange(BINS)
    frequency = bin_ids.astype(jnp.float32) * (SAMPLE_RATE / SAMPLES)
    over_white, full_weight = (
        lax.all_gather(over_local, "bank", axis=1, tiled=True),
        lax.all_gather(weight_sq, "bank", axis=0, tiled=True),
    )

    def norm_of(envelope):
        return jnp.sum(envelope * envelope * full_weight)

    tables = transform_tables()

    def filter_one(table_index):
        seconds, sym_ratio, orbit_term = template_terms(table_index)
        envelope = jnp.where(bin_ids >= LOW_BIN, amplitude(seconds, frequency), 0.0)
        phase_angle = phase(seconds, sym_ratio, orbit_term, frequency)
        filtered = filter_template(over_white, envelope, phase_angle, tables)
        return (filtered / jnp.sqrt(norm_of(envelope))).astype(jnp.bfloat16)

    def filter_step(slot_id, series_buf):
        scaled_series = filter_one(indices[slot_id])
        return lax.dynamic_update_index_in_dim(series_buf, scaled_series, slot_id, 0)

    series_all = lax.fori_loop(
        0, counts[0], filter_step, jnp.zeros((tpl_slots, 2, SERIES), jnp.bfloat16)
    )
    det_index = lax.axis_index("det")
    half_window = WINDOW // 2
    span_len = half_window + 2 * DFT_ROWS
    gathered = lax.all_gather(series_all[None], "det", axis=0, tiled=True)
    first_win = lax.dynamic_slice_in_dim(gathered[0], det_index * half_window, span_len, 2)
    second_win = lax.dynamic_slice_in_dim(gathered[1], det_index * half_window, span_len, 2)
    return coherent_stat(
        first_win, second_win, DFT_ROWS, half_window, sky_delay, gain_near, gain_far
    )


def solution(mesh):
    return jax.shard_map(
        on_device,
        mesh=mesh,
        in_specs=(P("det", None, "bank"), P("det", "bank"), P("bank"), P("bank"), P(), P(), P()),
        out_specs=P("bank", None, "det"),
        check_vma=False,
    )
```

profile of v0, /device:TPU:9, one launch (start us, length us, event | category | flops | bytes accessed | tf_op | source)
XLA Modules:
  0.0 1564.0 jit_solution(4272732596622240692)
XLA Ops:
  3.1 538.3 %all-gather = f32[1,65536]{1,0:T(1,128)S(1)} all-gather(f32[1,256]{1,0:T(1,128)S(1)} %mul.620), channel_id=2, replica_groups=mesh['bank'=256,'det'=2] {'bank'}, dimensions={1}, use_global_device_ids=true | all-gather | bytes 263168 | tf_op jit(solution)/shard_map/all_gather | solution.py:122
  541.4 2.0 fusion.61
  543.4 566.7 %all_gather.9 = f32[2,65536]{1,0:T(2,128)S(1)} all-gather(f32[2,256]{1,0:T(2,128)S(1)} %bitcast_multiply_fusion), channel_id=1, replica_groups=mesh['bank'=256,'det'=2] {'bank'}, dimensions={1}, use_global_device_ids=true | all-gather | bytes 526336 | tf_op jit(solution)/shard_map/all_gather | solution.py:121
  1110.1 2.2 sine_convert_fusion
  1113.3 199.0 %while.19 = (s32[]{:T(128)}, bf16[16,2,5120]{2,1,0:T(2,128)(2,1)}, s32[]{:T(128)}, f32[2,65536]{1,0:T(2,128)S(1)}, s32[16]{0:T(128)S(1)}, /*index=5*/bf16[1024,5...) while((s32[]{:T(128)}, bf16[16,2,5120]{2,1,0:T(2,128)(2,1)}, ...), condition=%wide.region_2.3_spmd.clone.clone, body=%wide.region_0.2_spmd.clone.clone.sunk | while | flops 286488640 | bytes 11297754 | solution.py:141
  1120.0 1.4 slice_reduce_fusion.3
  1123.3 2.3 subtract_convert_fusion.5
  1133.2 1.4 slice_reduce_fusion.3
  1136.5 2.3 subtract_convert_fusion.5
  1146.5 1.4 slice_reduce_fusion.3
  1149.7 2.3 subtract_convert_fusion.5
  1159.7 1.4 slice_reduce_fusion.3
  1163.0 2.3 subtract_convert_fusion.5
  1172.9 1.4 slice_reduce_fusion.3
  1176.2 2.3 subtract_convert_fusion.5
  1186.1 1.4 slice_reduce_fusion.3
  1189.4 2.3 subtract_convert_fusion.5
  1199.3 1.4 slice_reduce_fusion.3
  1202.6 2.3 subtract_convert_fusion.5
  1215.8 2.3 subtract_convert_fusion.5
  1229.1 2.3 subtract_convert_fusion.5
  1242.3 2.3 subtract_convert_fusion.5
  1252.2 1.4 slice_reduce_fusion.3
  1255.5 2.3 subtract_convert_fusion.5
  1268.7 2.3 subtract_convert_fusion.5
  1281.9 2.3 subtract_convert_fusion.5
  1291.9 1.4 slice_reduce_fusion.3
  1295.2 2.3 subtract_convert_fusion.5
  1308.4 2.3 subtract_convert_fusion.5
  1312.3 223.6 %all-gather.1 = bf16[32,2,5120]{2,1,0:T(2,128)(2,1)S(1)} all-gather(bf16[16,2,5120]{2,1,0:T(2,128)(2,1)} %get-tuple-element.326), channel_id=3, replica_groups=mesh['bank'=256,'det'=2] {'det'}, dimensions={0}, use_global_device_ids=true | all-gather | bytes 983040 | tf_op jit(solution)/shard_map/all_gather | solution.py:147
  1537.0 23.7 %while.18 = (s32[]{:T(128)}, bf16[16,2,3072]{2,1,0:T(2,128)(2,1)S(1)}, s32[16,3]{0,1:T(4,128)S(1)}, bf16[16,16,2,2048]{3,2,1,0:T(2,128)(2,1)S(1)}, s32[]{:T(128)}) while((s32[]{:T(128)}, bf16[16,2,3072]{2,1,0:T(2,128)(2,1)S(1)}, s32[16,3]{0,1:T(4,128)S(1)}, bf16[16,16,2,2048]{3,2,1,0:T(2,128)(2,1)S(1)}, s32[]{:T(128)}) %tuple.76), condition=%wide.while_cond, body=%wide.while_body.sunk | while | flops 2 | bytes 262257 | solution.py:102
  1561.9 2.1 fusion.51
  (349 shorter events, 115.0 us)
Async XLA Ops:
  0.0 1113.3 %copy-start.2 = (s32[16]{0:T(128)S(1)}, s32[16]{0:T(128)}, u32[]{:S(2)}) copy-start(s32[16]{0:T(128)} %param.11) | copy-start | bytes 196
  1560.7 1.3 copy-start
  1560.7 1.3 copy-start.1
where the time goes:
time: 1570 us; the launch traced here: 1560 us
  blocking collectives  1330 us (85%)
  other arithmetic  94.9 us (6%)
  loops' own time  67.4 us (4%)
  local copies, waits for them, and re-layouts  63.2 us (4%)
    all_gather x1, blocking collectives, on_device(): lax.all_gather(over_local, 'bank', axis=1, tiled=True)  567 us
    all_gather x1, blocking collectives, on_device(): lax.all_gather(weight_sq, 'bank', axis=0, tiled=True)  538 us
    all_gather x1, blocking collectives, on_device(): gathered = lax.all_gather(series_all[None], 'det', axis=0, tiled=True)  224 us
    another operation x1, loops' own time, on_device(): lax.fori_loop(0, counts[0], filter_step, jnp.zeros((tpl_slots, 2, SERIES)...  67.2 us
    another operation x30, other arithmetic  53 us

commit v1 on v0

v1 whole, which is shorter than its diff:
```python
import math

import jax
import jax.numpy as jnp
import numpy as np
from jax import lax
from jax.experimental import pallas as pl
from jax.experimental.pallas import tpu as pltpu
from jax.sharding import PartitionSpec as P

DFT_ROWS = 512
DFT_COLS = 256
SAMPLES = 131072
LOW_BIN = 1920
WIN_BLOCKS = 8
WINDOW = 4096
HALF = WINDOW // 2
TPL_DEV = 16
SKY = 16
MASSES = 64
N_Z = 16
N_XY = 16
COLS = WIN_BLOCKS + 2
SPAN = HALF + 256
PAYLOAD = 640
STRIP = 32
TIME_BLOCK = 512

MSUN_SEC = 4.925491e-06
SAMPLE_RATE = 2048.0

Z_ORDER = [8, 10, 12, 14, 0, 2, 4, 6, 9, 11, 13, 15, 1, 3, 5, 7]
XY_ORDER = [(k + 5) % N_XY for k in range(N_XY)]


def group_lists():
    z_groups = [[q * N_Z + z for z in Z_ORDER] for q in range(N_XY)]
    xy_groups = [[q * N_Z + z for q in XY_ORDER] for z in range(N_Z)]
    return z_groups, xy_groups


def constant_tables():
    rows = np.array([[q * N_Z + z for z in Z_ORDER] for q in XY_ORDER])
    even, odd = rows[:, :8].reshape(-1), rows[:, 8:].reshape(-1)
    k1 = np.concatenate([even, odd])
    k2 = np.arange(DFT_COLS)
    bins = 256 * k1[None, :] + k2[:, None]
    freq = np.maximum(bins * (SAMPLE_RATE / SAMPLES), 1.0)
    powers = np.stack(
        [
            freq ** (-5.0 / 3.0),
            freq**-1.0,
            freq ** (-2.0 / 3.0),
            np.where(bins >= LOW_BIN, freq ** (-7.0 / 6.0), 0.0),
            freq**4,
        ]
    ).astype(np.float32)

    t1 = np.arange(256)

    def first(rows_k):
        angle = 2.0 * np.pi / 512 * (rows_k[:, None] * t1[None, :] % 512)
        c, s = np.cos(angle), np.sin(angle)
        return np.concatenate([np.concatenate([c, s], 1), np.concatenate([-s, c], 1)], 0)

    first_tables = np.stack([first(even), first(odd)])
    t_all = np.arange(512)
    angle = 2.0 * np.pi / SAMPLES * (k2[:, None] * t_all[None, :] % SAMPLES)
    twist = np.stack([np.cos(angle), np.sin(angle)]).astype(np.float32)
    t2 = DFT_COLS // 2 - WIN_BLOCKS // 2 - 1 + np.arange(COLS)
    angle = 2.0 * np.pi / DFT_COLS * (t2[:, None] * k2[None, :] % DFT_COLS)
    c, s = np.cos(angle), np.sin(angle)
    last = np.zeros((32, 512))
    last[:COLS] = np.concatenate([c, -s], 1)
    last[COLS : 2 * COLS] = np.concatenate([s, c], 1)

    seconds = 6.0 * 1.03 ** np.arange(MASSES) * MSUN_SEC
    ratio = 0.16 + 0.09 * np.arange(64) / 63.0
    x = np.pi * seconds
    turn = 1.0 / (2.0 * np.pi)
    scalars = np.stack(
        [
            turn * x ** (-5.0 / 3.0),
            turn * x**-1.0,
            turn * x ** (-2.0 / 3.0),
            -((6.0**1.5 * x) ** 4) / math.log(2.0),
            3.0 / (128.0 * ratio),
            3715.0 / 756.0 + 55.0 * ratio / 9.0,
            (113.0 - 76.0 * ratio) / 12.0,
            np.zeros(64),
        ]
    ).astype(np.float32)
    return (
        powers,
        first_tables.astype(jnp.bfloat16),
        twist,
        last.astype(jnp.bfloat16),
        scalars,
    )


def even_fit(function, terms):
    nodes = 0.5 * np.cos(np.pi * (np.arange(400) + 0.5) / 400)
    design = (nodes[:, None] ** 2) ** np.arange(terms)[None, :]
    fitted = np.linalg.lstsq(design, function(nodes), rcond=None)[0]
    return [float(np.float32(v)) for v in fitted]


ROOT2 = math.sqrt(2.0)
SIN_FIT = even_fit(lambda r: ROOT2 * np.pi * np.sinc(r), 5)
COS_FIT = even_fit(lambda r: ROOT2 * np.cos(np.pi * r), 5)
ROUND_SHIFT = 12582912.0


def horner(coefs, square):
    total = coefs[-1] * square + coefs[-2]
    for c in coefs[-3::-1]:
        total = total * square + c
    return total


def prepare_kernel(bank_ref, strain_ref, asd_ref, out_ref):
    weight = asd_ref[...] * asd_ref[...]
    over = strain_ref[...] * weight
    bin_id = bank_ref[0] * 256 + lax.broadcasted_iota(jnp.int32, (1, 256), 1)
    clipped = jnp.maximum(bin_id.astype(jnp.float32) * (SAMPLE_RATE / SAMPLES), 1.0)
    square = clipped * clipped
    weighted = jnp.where(
        bin_id >= LOW_BIN, jnp.exp((-7.0 / 3.0) * jnp.log(clipped)), 0.0
    ) * weight
    mass_id = lax.broadcasted_iota(jnp.int32, (MASSES, 1), 0).astype(jnp.float32)
    start = math.log(2.0) + 4.0 * math.log(6.0**1.5 * math.pi * 6.0 * MSUN_SEC)
    steep = jnp.exp(4.0 * math.log(1.03) * mass_id + start)
    terms = jnp.exp(-steep * (square * square)) * weighted
    column = jnp.sum(terms, axis=1, keepdims=True)
    row_id = lax.broadcasted_iota(jnp.int32, (MASSES, MASSES), 0)
    col_id = lax.broadcasted_iota(jnp.int32, (MASSES, MASSES), 1)
    norms = jnp.sum(jnp.where(row_id == col_id, column, 0.0), axis=0, keepdims=True)
    coarse = norms.astype(jnp.bfloat16).astype(jnp.float32)
    row = jnp.concatenate(
        [over[0:1].astype(jnp.bfloat16).astype(jnp.float32), over[1:2].astype(jnp.bfloat16).astype(jnp.float32), coarse, norms - coarse], axis=1
    )
    out_ref[...] = jnp.broadcast_to(row[:, None, :], (N_Z, 1, PAYLOAD))


def filter_kernel(
    indices_ref,
    counts_ref,
    half_ref,
    scalars_ref,
    gathered_ref,
    powers_ref,
    first_ref,
    twist_ref,
    last_ref,
    own_ref,
    send_ref,
    spectrum,
    products,
    middle,
    twisted,
    series,
):
    count = counts_ref[0]
    for part in range(2):
        block = gathered_ref[:, :, 256 * part : 256 * part + 256].astype(jnp.float32)
        for parity in range(2):
            rows = block[:, 8 * parity : 8 * parity + 8].reshape(128, 256)
            spectrum[part, :, 128 * parity : 128 * parity + 128] = rows.T
    sums = jnp.sum(gathered_ref[:, :, 512:640].astype(jnp.float32).reshape(256, 128), axis=0, keepdims=True)
    norm_row = sums[:, :MASSES] + sums[:, MASSES:]
    lane_id = lax.broadcasted_iota(jnp.int32, (1, MASSES), 1)
    series[...] = jnp.zeros_like(series)

    @pl.loop(0, count)
    def _(slot):
        entry = indices_ref[slot]
        mass, eta = entry % 64, entry // 64 % 64
        spin = -0.6 + 0.4 * (entry // 4096).astype(jnp.float32)
        lead = scalars_ref[4, eta]
        c53 = lead * scalars_ref[0, mass]
        c1 = lead * scalars_ref[5, eta] * scalars_ref[1, mass]
        c23 = lead * (4.0 * spin * scalars_ref[6, eta] - 16.0 * math.pi) * scalars_ref[2, mass]
        steep = scalars_ref[3, mass]
        norm = jnp.sum(jnp.where(lane_id == mass, norm_row, 0.0), axis=1, keepdims=True)
        scale = lax.rsqrt(norm)

        @pl.loop(0, DFT_COLS // STRIP)
        def _(strip):
            here = pl.ds(pl.multiple_of(strip * STRIP, STRIP), STRIP)
            turns = (
                c53 * powers_ref[0, here, :]
                + c1 * powers_ref[1, here, :]
                + (c23 * powers_ref[2, here, :] - 0.125)
            )
            rest = turns - ((turns + ROUND_SHIFT) - ROUND_SHIFT)
            square = rest * rest
            half_sin = horner(SIN_FIT, square) * rest
            half_cos = horner(COS_FIT, square)
            envelope = powers_ref[3, here, :] * jnp.exp2(steep * powers_ref[4, here, :])
            sine = envelope * (half_sin * half_cos)
            cosine = envelope * (1.0 - half_sin * half_sin)
            re, im = spectrum[0, here, :], spectrum[1, here, :]
            real_part = (re * cosine - im * sine).astype(jnp.bfloat16)
            imag_part = (re * sine + im * cosine).astype(jnp.bfloat16)
            for parity in range(2):
                lanes = slice(128 * parity, 128 * parity + 128)
                products[parity, here, 0:128] = real_part[:, lanes]
                products[parity, here, 128:256] = imag_part[:, lanes]

        for parity in range(2):
            middle[parity] = jnp.dot(
                products[parity], first_ref[parity], preferred_element_type=jnp.float32
            )

        @pl.loop(0, DFT_COLS // STRIP)
        def _(strip):
            base = pl.multiple_of(strip * STRIP, STRIP)
            here, below = pl.ds(base, STRIP), pl.ds(base + DFT_COLS, STRIP)
            for side in range(2):
                lanes = slice(256 * side, 256 * side + 256)
                if side == 0:
                    upper = middle[0, here, 0:256] + middle[1, here, 0:256]
                    lower = middle[0, here, 256:512] + middle[1, here, 256:512]
                else:
                    upper = middle[0, here, 0:256] - middle[1, here, 0:256]
                    lower = middle[0, here, 256:512] - middle[1, here, 256:512]
                c, s = twist_ref[0, here, lanes], twist_ref[1, here, lanes]
                twisted[here, lanes] = (upper * c - lower * s).astype(jnp.bfloat16)
                twisted[below, lanes] = (upper * s + lower * c).astype(jnp.bfloat16)

        result = jnp.dot(last_ref[...], twisted[...], preferred_element_type=jnp.float32)
        scaled = result[: 2 * COLS] * scale
        for i in range(4):
            series[i, pl.ds(slot, 2 * COLS, stride=TPL_DEV), :] = scaled[:, 128 * i : 128 * i + 128]

    def write(out_ref, half):
        for part in range(2):
            start = (part * COLS + 4 * half) * TPL_DEV

            def rows(column):
                return pl.ds(pl.multiple_of(start + column * TPL_DEV, TPL_DEV), TPL_DEV)

            for i in range(SPAN // 128):
                column, tile = divmod(i + 3, 4)
                out_ref[part, :, 128 * i : 128 * i + 128] = series[tile, rows(column), :].astype(
                    jnp.bfloat16
                )

    write(own_ref, half_ref[0])
    write(send_ref, 1 - half_ref[0])


def coherent_kernel(half_ref, delay_ref, near_gain_ref, far_gain_ref, own_ref, got_ref, out_ref, near, far, tiles):
    block = pl.program_id(0)

    def unpack(near_ref, far_ref):
        for part in range(2):
            near[part] = near_ref[part, :, 128 : 128 + HALF].astype(jnp.float32)
            far[part] = far_ref[part].astype(jnp.float32)[:, 64 : 64 + HALF + 128]

    @pl.when((block == 0) & (half_ref[0] == 0))
    def _():
        unpack(own_ref, got_ref)

    @pl.when((block == 0) & (half_ref[0] == 1))
    def _():
        unpack(got_ref, own_ref)

    lane_id = lax.broadcasted_iota(jnp.int32, (TPL_DEV, 128), 1)
    first_lane = pl.multiple_of(block * TIME_BLOCK, 128)

    @pl.loop(0, SKY)
    def _(sky):
        shift = delay_ref[sky] + 64
        gain_near = near_gain_ref[sky]
        gain_far = far_gain_ref[sky]
        power = jnp.full((1, 128), gain_near * gain_near + gain_far * gain_far, jnp.float32)
        inverse = 1.0 / power
        keep = lane_id < 128 - shift
        total = [None] * (TIME_BLOCK // 128)
        for part in range(2):
            rolled = [
                pltpu.roll(far[part, :, pl.ds(first_lane + 128 * i, 128)], 128 - shift, axis=1)
                for i in range(TIME_BLOCK // 128 + 1)
            ]
            for i in range(TIME_BLOCK // 128):
                shifted = jnp.where(keep, rolled[i], rolled[i + 1])
                mixed = (
                    gain_near * near[part, :, pl.ds(first_lane + 128 * i, 128)] + gain_far * shifted
                )
                squared = mixed * mixed
                total[i] = squared if part == 0 else total[i] + squared
        for i in range(TIME_BLOCK // 128):
            tiles[i, pl.ds(sky, TPL_DEV, stride=SKY), :] = total[i] * inverse

    for i in range(TIME_BLOCK // 128):
        out_ref[:, 128 * i : 128 * i + 128] = tiles[i]


VMEM = pl.BlockSpec(memory_space=pltpu.VMEM)
SMEM = pl.BlockSpec(memory_space=pltpu.SMEM)


def on_device(strain, asd_inv, indices, counts, sky_delay, gain_near, gain_far):
    powers, first_tables, twist, last, scalars = constant_tables()
    z_groups, xy_groups = group_lists()
    bank = lax.axis_index("bank").astype(jnp.int32)[None]
    half = lax.axis_index("det").astype(jnp.int32)[None]
    payload = pl.pallas_call(
        prepare_kernel,
        out_shape=jax.ShapeDtypeStruct((N_Z, 1, PAYLOAD), jnp.float32),
        in_specs=[SMEM, VMEM, VMEM],
        out_specs=VMEM,
    )(bank, strain[0], asd_inv)
    line = lax.all_to_all(payload, "bank", 0, 0, axis_index_groups=z_groups)
    line = line.reshape(N_Z, PAYLOAD).astype(jnp.bfloat16)
    plane = lax.all_to_all(
        jnp.broadcast_to(line[None], (N_XY, N_Z, PAYLOAD)), "bank", 0, 0, axis_index_groups=xy_groups
    )
    window = jax.ShapeDtypeStruct((2, TPL_DEV, SPAN), jnp.bfloat16)
    own, send = pl.pallas_call(
        filter_kernel,
        out_shape=(window, window),
        in_specs=[SMEM] * 4 + [VMEM] * 5,
        out_specs=(VMEM, VMEM),
        scratch_shapes=[
            pltpu.VMEM((2, DFT_COLS, 256), jnp.float32),
            pltpu.VMEM((2, DFT_COLS, 256), jnp.bfloat16),
            pltpu.VMEM((2, DFT_COLS, 512), jnp.float32),
            pltpu.VMEM((512, 512), jnp.bfloat16),
            pltpu.VMEM((4, 2 * COLS * TPL_DEV, 128), jnp.float32),
        ],
        compiler_params=pltpu.CompilerParams(vmem_limit_bytes=40 * 1024 * 1024),
    )(indices, counts, half, scalars, plane, powers, first_tables, twist, last)
    got = lax.ppermute(send, "det", [(0, 1), (1, 0)])
    out = pl.pallas_call(
        coherent_kernel,
        grid=(HALF // TIME_BLOCK,),
        out_shape=jax.ShapeDtypeStruct((TPL_DEV * SKY, HALF), jnp.float32),
        in_specs=[SMEM] * 4 + [VMEM] * 2,
        out_specs=pl.BlockSpec((TPL_DEV * SKY, TIME_BLOCK), lambda t: (0, t)),
        scratch_shapes=[
            pltpu.VMEM((2, TPL_DEV, HALF), jnp.float32),
            pltpu.VMEM((2, TPL_DEV, HALF + 128), jnp.float32),
            pltpu.VMEM((TIME_BLOCK // 128, TPL_DEV * SKY, 128), jnp.float32),
        ],
        compiler_params=pltpu.CompilerParams(vmem_limit_bytes=40 * 1024 * 1024),
    )(half, sky_delay, gain_near, gain_far, own, got)
    return out.reshape(TPL_DEV, SKY, HALF)


def solution(mesh):
    return jax.shard_map(
        on_device,
        mesh=mesh,
        in_specs=(P("det", None, "bank"), P("det", "bank"), P("bank"), P("bank"), P(), P(), P()),
        out_specs=P("bank", None, "det"),
        check_vma=False,
    )
```

time: 1570 us -> 75.9 us (0.05)
  the two profiles are of different devices: /device:TPU:9 before, /device:TPU:129 now
where the time goes in v1:
time: 75.9 us; the launch traced here: 75.4 us
  Pallas kernels  29.5 us (39%)
  blocking collectives  18.5 us (24%)
  starting transfers between devices  11.9 us (16%)
  waiting for transfers between devices  7.21 us (9%)
  local copies, waits for them, and re-layouts  5.86 us (8%)
  other arithmetic  1.56 us (2%)
    pallas_call x1, Pallas kernels, on_device(): pl.pallas_call(filter_kernel, out_shape=(window, window), in_specs=[SMEM]...  19.4 us
    all_to_all x1, blocking collectives, on_device(): line = lax.all_to_all(payload, 'bank', 0, 0, axis_index_groups=z_groups)  18.5 us
    pallas_call x1, Pallas kernels, on_device(): pl.pallas_call(coherent_kernel, grid=(HALF // TIME_BLOCK,), out_shape=jax...  8.57 us
    all_to_all x1, starting transfers between devices, on_device(): lax.all_to_all(jnp.broadcast_to(line[None], (N_XY, N_Z, PAYLOAD)), 'bank'...  7.09 us
    all_to_all x1, waiting for transfers between devices, on_device(): lax.all_to_all(jnp.broadcast_to(line[None], (N_XY, N_Z, PAYLOAD)), 'bank'...  6.22 us
    unnamed x22, local copies, waits for them, and re-layouts  5.11 us
    ppermute x1, starting transfers between devices, on_device(): got = lax.ppermute(send, 'det', [(0, 1), (1, 0)])  4.86 us
    pallas_call x1, Pallas kernels, on_device(): pl.pallas_call(prepare_kernel, out_shape=jax.ShapeDtypeStruct((N_Z, 1, PA...  1.61 us
  transfers between devices with their start and end apart: 2, of which 2 were waited for; matrix products, arithmetic and copies ran while one was open for 0% of the time, Pallas kernels for 0%

profile of v1, /device:TPU:129, one launch (start us, length us, event | category | flops | bytes accessed | tf_op | source)
XLA Modules:
  0.0 75.4 jit_solution(4543554615160234508)
XLA Ops:
  0.0 0.0 copy-start
  0.0 1.6 %shard_map.118 = f32[16,1,640]{2,1,0:T(1,128)} custom-call(s32[1]{0:T(128)} %bitcast.1.bank_ref, f32[2,256]{1,0:T(2,128)} %bitcast.8, f32[1,256]{1,0:T(1,128)} %asd_ref.1), custom_call_target="tpu_custom_call" | custom-call | tf_op jit(solution)/shard_map/pallas_call | solution.py:310
  1.6 0.8 %convert = bf16[16,1,640]{2,1,0:T(2,128)(2,1)S(1)} convert(f32[16,1,640]{2,1,0:T(1,128)} %shard_map.118) | non-fusion elementwise | flops 10240 | bytes 61440
  2.4 0.5 broadcast
  2.9 0.8 %reduce = bf16[16,640]{1,0:T(8,128)(2,1)S(1)} reduce(bf16[16,1,640]{2,1,0:T(2,128)(2,1)S(1)} %convert, bf16[]{:T(256)} %broadcast), dimensions={1}, to_apply=%convert.reduce_sub_computation | reduce | bytes 40962
  3.7 0.1 reshape.11
  3.8 18.5 %all_to_all.10 = bf16[16,2,320]{2,1,0:T(2,128)(2,1)S(1)} all-to-all(bf16[16,2,320]{2,1,0:T(2,128)(2,1)S(1)} %reshape.11), channel_id=1, replica_groups={{16,20,24,28,0,4,8,12,18,22,26,30,2,6,10,14},{48,52,56,60,32,36,40,44,5..., dimensions={0} | all-to-all | bytes 40960 | tf_op jit(solution)/shard_map/all_to_all | solution.py:316
  22.3 0.1 reshape.12
  22.4 0.0 copy-start.6
  22.4 0.0 copy-start.7
  22.5 0.0 copy-start.8
  22.5 0.8 broadcast_in_dim.14
  23.2 7.1 %all-to-all-start.1 = ((bf16[16,16,640]{2,1,0:T(8,128)(2,1)}), bf16[16,16,640]{2,1,0:T(8,128)(2,1)S(1)}, u32[]{:S(2)}, u32[]{:S(2)}) async-start(bf16[16,16,640]{2,1,0:T(8,128)(2,1)} %broadcast_in_dim.14), calls=%async_computation.1 | async-start | bytes 655360 | tf_op jit(solution)/shard_map/all_to_all | solution.py:318
  31.0 6.2 %all-to-all-done.1.gathered_ref = bf16[16,16,640]{2,1,0:T(8,128)(2,1)S(1)} async-done(((bf16[16,16,640]{2,1,0:T(8,128)(2,1)}), bf16[16,16,640]{2,1,0:T(8,128)(2,1)S(1)}, u32[]{:S(2)}, u32[]{:S(2)}) %all-to-all-start.1) | async-done | bytes 327712 | tf_op jit(solution)/shard_map/all_to_all | solution.py:318
  37.2 0.0 copy-done
  37.2 0.0 copy-start.1
  37.2 1.2 %copy-done.1 = f32[2,256,512]{2,1,0:T(8,128)S(1)} copy-done((f32[2,256,512]{2,1,0:T(8,128)S(1)}, f32[2,256,512]{2,1,0:T(8,128)}, u32[]{:S(2)}) %copy-start.1) | copy-done | bytes 1048600
  38.4 0.0 copy-start.2
  38.4 1.0 %copy-done.2 = bf16[2,256,512]{2,1,0:T(8,128)(2,1)S(1)} copy-done((bf16[2,256,512]{2,1,0:T(8,128)(2,1)S(1)}, bf16[2,256,512]{2,1,0:T(8,128)(2,1)}, u32[]{:S(2)}) %copy-start.2) | copy-done | bytes 524312
  39.5 0.0 copy-start.3
  39.5 0.8 %copy-done.3 = bf16[32,512]{1,0:T(8,128)(2,1)S(1)} copy-done((bf16[32,512]{1,0:T(8,128)(2,1)S(1)}, bf16[32,512]{1,0:T(8,128)(2,1)}, u32[]{:S(2)}) %copy-start.3) | copy-done | bytes 32792
  40.2 0.0 copy-start.4
  40.2 0.7 copy-done.4
  40.9 0.0 copy-start.5
  40.9 0.7 copy-done.5
  41.6 19.4 %shard_map.119 = (bf16[2,16,2304]{2,1,0:T(8,128)(2,1)S(1)}, bf16[2,16,2304]{2,1,0:T(8,128)(2,1)S(1)}) custom-call(s32[16]{0:T(128)S(1)} %copy-done.5, s32[1]{0:T(128)S(6)} %copy.16.counts_ref, s32[1]{0:T(128)} %bitcast.half_ref, f32[8,64]{1,0:T(8,128)S(1)} %copy-done.4, bf16[16,16,640]{2,1,0:T(8,128)(2,1)S(1)} %all-to-all-done.1.gathered_ref, ...), custom_call_target="tpu_custom_call" | custom-call | tf_op jit(solution)/shard_map/pallas_call | solution.py:322
  60.9 4.9 %collective-permute-start = (bf16[2,16,2304]{2,1,0:T(8,128)(2,1)S(1)}, bf16[2,16,2304]{2,1,0:T(8,128)(2,1)S(1)}, u32[]{:S(2)}, u32[]{:S(2)}) collective-permute-start(bf16[2,16,2304]{2,1,0:T(8,128)(2,1)S(1)} %get-tuple-element.8), channel_id=1, source_target_pairs={{0,1},{1,0},{2,3},{3,2},{4,5},{5,4},{6,7},{7,6},{8,9},{9,8},{10,11... | collective-permute-start | bytes 442376 | tf_op jit(solution)/shard_map/ppermute | solution.py:336
  65.8 1.0 %collective-permute-done.got_ref = bf16[2,16,2304]{2,1,0:T(8,128)(2,1)S(1)} collective-permute-done((bf16[2,16,2304]{2,1,0:T(8,128)(2,1)S(1)}, bf16[2,16,2304]{2,1,0:T(8,128)(2,1)S(1)}, u32[]{:S(2)}, u32[]{:S(2)}) %collective-permute-start) | collective-permute-done | bytes 147488 | tf_op jit(solution)/shard_map/ppermute | solution.py:336
  66.8 0.0 copy-done.6
  66.8 0.0 copy-done.7
  66.8 0.0 copy-done.8
  66.8 8.6 %shard_map.120 = f32[256,2048]{1,0:T(8,128)} custom-call(s32[1]{0:T(128)} %bitcast.half_ref, s32[16]{0:T(128)S(1)} %copy-done.6, f32[16]{0:T(128)S(1)} %copy-done.7, f32[16]{0:T(128)S(1)} %copy-done.8, bf16[2,16,2304]{2,1,0:T(8,128)(2,1)S(1)} %get-tuple-element.7.own_ref, bf16[2,16,2304]{2,1,0:T(8,128)(2,1)S(1)} %collective-permute-done.got_ref), custom_call_target="tpu_custom_call" | custom-call | tf_op jit(solution)/shard_map/pallas_call | solution.py:337
  (1 shorter events, 0.0 us)
Async XLA Ops:
  0.0 37.2 %copy-start = (f32[5,256,256]{2,1,0:T(8,128)S(1)}, f32[5,256,256]{2,1,0:T(8,128)}, u32[]{:S(2)}) copy-start(f32[5,256,256]{2,1,0:T(8,128)} %constant.19.clone.powers_ref) | copy-start | bytes 3932164
  22.4 44.3 %copy-start.6 = (s32[16]{0:T(128)S(1)}, s32[16]{0:T(128)}, u32[]{:S(2)}) copy-start(s32[16]{0:T(128)} %delay_ref.1) | copy-start | bytes 196
  22.4 44.3 %copy-start.7 = (f32[16]{0:T(128)S(1)}, f32[16]{0:T(128)}, u32[]{:S(2)}) copy-start(f32[16]{0:T(128)} %near_gain_ref.1) | copy-start | bytes 196
  22.5 44.3 %copy-start.8 = (f32[16]{0:T(128)S(1)}, f32[16]{0:T(128)}, u32[]{:S(2)}) copy-start(f32[16]{0:T(128)} %far_gain_ref.1) | copy-start | bytes 196
  23.2 14.0 %all-to-all-start.1 = ((bf16[16,16,640]{2,1,0:T(8,128)(2,1)}), bf16[16,16,640]{2,1,0:T(8,128)(2,1)S(1)}, u32[]{:S(2)}, u32[]{:S(2)}) async-start(bf16[16,16,640]{2,1,0:T(8,128)(2,1)} %broadcast_in_dim.14), calls=%async_computation.1 | async-start | bytes 655360 | tf_op jit(solution)/shard_map/all_to_all | solution.py:318
  37.2 1.2 %copy-start.1 = (f32[2,256,512]{2,1,0:T(8,128)S(1)}, f32[2,256,512]{2,1,0:T(8,128)}, u32[]{:S(2)}) copy-start(f32[2,256,512]{2,1,0:T(8,128)} %constant.21.clone.twist_ref) | copy-start | bytes 3145732
  38.4 1.0 %copy-start.2 = (bf16[2,256,512]{2,1,0:T(8,128)(2,1)S(1)}, bf16[2,256,512]{2,1,0:T(8,128)(2,1)}, u32[]{:S(2)}) copy-start(bf16[2,256,512]{2,1,0:T(8,128)(2,1)} %constant.20.clone.first_ref) | copy-start | bytes 1572868
  39.5 0.8 %copy-start.3 = (bf16[32,512]{1,0:T(8,128)(2,1)S(1)}, bf16[32,512]{1,0:T(8,128)(2,1)}, u32[]{:S(2)}) copy-start(bf16[32,512]{1,0:T(8,128)(2,1)} %constant.22.clone.last_ref) | copy-start | bytes 98308
  40.2 0.7 copy-start.4
  40.9 0.7 copy-start.5
  60.9 5.8 %collective-permute-start = (bf16[2,16,2304]{2,1,0:T(8,128)(2,1)S(1)}, bf16[2,16,2304]{2,1,0:T(8,128)(2,1)S(1)}, u32[]{:S(2)}, u32[]{:S(2)}) collective-permute-start(bf16[2,16,2304]{2,1,0:T(8,128)(2,1)S(1)} %get-tuple-element.8), channel_id=1, source_target_pairs={{0,1},{1,0},{2,3},{3,2},{4,5},{5,4},{6,7},{7,6},{8,9},{9,8},{10,11... | collective-permute-start | bytes 442376 | tf_op jit(solution)/shard_map/ppermute | solution.py:336

commit v2 on v1

v2 whole, which is shorter than its diff:
```python
import math

import jax
import jax.numpy as jnp
import numpy as np
from jax import lax
from jax.experimental import pallas as pl
from jax.experimental.pallas import tpu as pltpu
from jax.sharding import PartitionSpec as P

DFT_ROWS = 512
DFT_COLS = 256
SAMPLES = 131072
LOW_BIN = 1920
WIN_BLOCKS = 8
WINDOW = 4096
HALF = WINDOW // 2
TPL_DEV = 16
SKY = 16
MASSES = 64
N_Z = 16
N_XY = 16
COLS = WIN_BLOCKS + 2
SPAN = HALF + 256
PAYLOAD = 640
STRIP = 16
BATCH = 4
TILES = HALF // 128
GROUP = 4

MSUN_SEC = 4.925491e-06
SAMPLE_RATE = 2048.0

Z_ORDER = [8, 10, 12, 14, 0, 2, 4, 6, 9, 11, 13, 15, 1, 3, 5, 7]
XY_ORDER = [(k + 5) % N_XY for k in range(N_XY)]


def group_lists():
    z_groups = [[q * N_Z + z for z in Z_ORDER] for q in range(N_XY)]
    xy_groups = [[q * N_Z + z for q in XY_ORDER] for z in range(N_Z)]
    return z_groups, xy_groups


def constant_tables():
    rows = np.array([[q * N_Z + z for z in Z_ORDER] for q in XY_ORDER])
    even, odd = rows[:, :8].reshape(-1), rows[:, 8:].reshape(-1)
    k1 = np.concatenate([even, odd])
    k2 = np.arange(DFT_COLS)
    bins = 256 * k1[None, :] + k2[:, None]
    freq = np.maximum(bins * (SAMPLE_RATE / SAMPLES), 1.0)
    powers = np.stack(
        [
            freq ** (-5.0 / 3.0),
            freq**-1.0,
            freq ** (-2.0 / 3.0),
            np.where(bins >= LOW_BIN, freq ** (-7.0 / 6.0), 0.0),
            freq**4,
        ]
    ).astype(np.float32)

    t1 = np.arange(256)

    def first(rows_k):
        angle = 2.0 * np.pi / 512 * (rows_k[:, None] * t1[None, :] % 512)
        c, s = np.cos(angle), np.sin(angle)
        return np.concatenate([np.concatenate([c, s], 1), np.concatenate([-s, c], 1)], 0)

    first_tables = np.stack([first(even), first(odd)])
    angle = 2.0 * np.pi / SAMPLES * (k2[:, None] * t1[None, :] % SAMPLES)
    twist = np.stack([np.cos(angle), np.sin(angle)]).astype(np.float32)
    t2 = DFT_COLS // 2 - WIN_BLOCKS // 2 - 1 + np.arange(COLS)
    last = np.zeros((2, 32, 512))
    for side in range(2):
        steps = k2[None, :] * (t2[:, None] * DFT_ROWS + 256 * side)
        angle = 2.0 * np.pi / SAMPLES * (steps % SAMPLES)
        c, s = np.cos(angle), np.sin(angle)
        last[side, :COLS] = np.concatenate([c, -s], 1)
        last[side, COLS : 2 * COLS] = np.concatenate([s, c], 1)

    seconds = 6.0 * 1.03 ** np.arange(MASSES) * MSUN_SEC
    ratio = 0.16 + 0.09 * np.arange(64) / 63.0
    x = np.pi * seconds
    turn = 1.0 / (2.0 * np.pi)
    scalars = np.stack(
        [
            turn * x ** (-5.0 / 3.0),
            turn * x**-1.0,
            turn * x ** (-2.0 / 3.0),
            -((6.0**1.5 * x) ** 4) / math.log(2.0),
            3.0 / (128.0 * ratio),
            3715.0 / 756.0 + 55.0 * ratio / 9.0,
            (113.0 - 76.0 * ratio) / 12.0,
            np.zeros(64),
        ]
    ).astype(np.float32)
    return (
        powers,
        first_tables.astype(jnp.bfloat16),
        twist,
        last.astype(jnp.bfloat16),
        scalars,
    )


def even_fit(function, terms):
    nodes = 0.5 * np.cos(np.pi * (np.arange(400) + 0.5) / 400)
    design = (nodes[:, None] ** 2) ** np.arange(terms)[None, :]
    fitted = np.linalg.lstsq(design, function(nodes), rcond=None)[0]
    return [float(np.float32(v)) for v in fitted]


ROOT2 = math.sqrt(2.0)
SIN_FIT = even_fit(lambda r: ROOT2 * np.pi * np.sinc(r), 5)
COS_FIT = even_fit(lambda r: ROOT2 * np.cos(np.pi * r), 5)
ROUND_SHIFT = 12582912.0


def horner(coefs, square):
    total = coefs[-1] * square + coefs[-2]
    for c in coefs[-3::-1]:
        total = total * square + c
    return total


def prepare_kernel(bank_ref, strain_ref, asd_ref, out_ref):
    weight = asd_ref[...] * asd_ref[...]
    over = strain_ref[...] * weight
    bin_id = bank_ref[0] * 256 + lax.broadcasted_iota(jnp.int32, (1, 256), 1)
    clipped = jnp.maximum(bin_id.astype(jnp.float32) * (SAMPLE_RATE / SAMPLES), 1.0)
    square = clipped * clipped
    weighted = jnp.where(
        bin_id >= LOW_BIN, jnp.exp((-7.0 / 3.0) * jnp.log(clipped)), 0.0
    ) * weight
    mass_id = lax.broadcasted_iota(jnp.int32, (MASSES, 1), 0).astype(jnp.float32)
    start = math.log(2.0) + 4.0 * math.log(6.0**1.5 * math.pi * 6.0 * MSUN_SEC)
    steep = jnp.exp(4.0 * math.log(1.03) * mass_id + start)
    terms = jnp.exp(-steep * (square * square)) * weighted
    column = jnp.sum(terms, axis=1, keepdims=True)
    row_id = lax.broadcasted_iota(jnp.int32, (MASSES, MASSES), 0)
    col_id = lax.broadcasted_iota(jnp.int32, (MASSES, MASSES), 1)
    norms = jnp.sum(jnp.where(row_id == col_id, column, 0.0), axis=0, keepdims=True)
    coarse = norms.astype(jnp.bfloat16).astype(jnp.float32)
    row = jnp.concatenate(
        [over[0:1].astype(jnp.bfloat16).astype(jnp.float32), over[1:2].astype(jnp.bfloat16).astype(jnp.float32), coarse, norms - coarse], axis=1
    )
    out_ref[...] = jnp.broadcast_to(row[:, None, :], (N_Z, 1, PAYLOAD))


def spread_kernel(line_ref, out_ref):
    line = line_ref[...].reshape(N_Z, PAYLOAD).astype(jnp.bfloat16)
    for i in range(N_XY):
        out_ref[i] = line


def wave_kernel(indices_ref, counts_ref, scalars_ref, powers_ref, waves_ref):
    @pl.loop(0, (counts_ref[0] + BATCH - 1) // BATCH * BATCH)
    def _(slot):
        entry = indices_ref[slot]
        mass, eta = entry % 64, entry // 64 % 64
        spin = -0.6 + 0.4 * (entry // 4096).astype(jnp.float32)
        lead = scalars_ref[4, eta]
        c53 = lead * scalars_ref[0, mass]
        c1 = lead * scalars_ref[5, eta] * scalars_ref[1, mass]
        c23 = lead * (4.0 * spin * scalars_ref[6, eta] - 16.0 * math.pi) * scalars_ref[2, mass]
        steep = scalars_ref[3, mass]

        @pl.loop(0, DFT_COLS // 64)
        def _(strip):
            for step in range(8):
                here = pl.ds(pl.multiple_of(strip * 64 + step * 8, 8), 8)
                turns = (
                    c53 * powers_ref[0, here, :]
                    + c1 * powers_ref[1, here, :]
                    + (c23 * powers_ref[2, here, :] - 0.125)
                )
                rest = turns - ((turns + ROUND_SHIFT) - ROUND_SHIFT)
                square = rest * rest
                half_sin = horner(SIN_FIT, square) * rest
                half_cos = horner(COS_FIT, square)
                envelope = powers_ref[3, here, :] * jnp.exp2(steep * powers_ref[4, here, :])
                waves_ref[slot, 0, here, :] = envelope * (1.0 - half_sin * half_sin)
                waves_ref[slot, 1, here, :] = envelope * (half_sin * half_cos)


def filter_kernel(
    indices_ref,
    counts_ref,
    half_ref,
    waves_ref,
    gathered_ref,
    first_ref,
    twist_ref,
    last_ref,
    own_ref,
    send_ref,
    spectrum,
    products,
    middle,
    twisted,
    series,
):
    count = counts_ref[0]
    for part in range(2):
        block = gathered_ref[:, :, 256 * part : 256 * part + 256].astype(jnp.float32)
        for parity in range(2):
            rows = block[:, 8 * parity : 8 * parity + 8].reshape(128, 256)
            spectrum[part, :, 128 * parity : 128 * parity + 128] = rows.T
    sums = jnp.sum(
        gathered_ref[:, :, 512:640].astype(jnp.float32).reshape(256, 128), axis=0, keepdims=True
    )
    norm_row = sums[:, :MASSES] + sums[:, MASSES:]
    lane_id = lax.broadcasted_iota(jnp.int32, (1, MASSES), 1)
    series[...] = jnp.zeros_like(series)

    def multiply(slot, place):
        for i in range(0, DFT_COLS, STRIP):
            here, there = slice(i, i + STRIP), slice(256 * place + i, 256 * place + i + STRIP)
            cosine, sine = waves_ref[slot, 0, here, :], waves_ref[slot, 1, here, :]
            re, im = spectrum[0, here, :], spectrum[1, here, :]
            real_part = (re * cosine - im * sine).astype(jnp.bfloat16)
            imag_part = (re * sine + im * cosine).astype(jnp.bfloat16)
            for parity in range(2):
                lanes = slice(128 * parity, 128 * parity + 128)
                products[parity, there, 0:128] = real_part[:, lanes]
                products[parity, there, 128:256] = imag_part[:, lanes]

    def twist(place):
        for i in range(0, DFT_COLS, STRIP):
            here, below = slice(i, i + STRIP), slice(256 + i, 256 + i + STRIP)
            there = slice(256 * place + i, 256 * place + i + STRIP)
            even_re, even_im = middle[0, there, 0:256], middle[0, there, 256:512]
            odd_re, odd_im = middle[1, there, 0:256], middle[1, there, 256:512]
            c, s = twist_ref[0, here, :], twist_ref[1, here, :]
            for side in range(2):
                lanes = slice(256 * side, 256 * side + 256)
                upper = even_re - odd_re if side else even_re + odd_re
                lower = even_im - odd_im if side else even_im + odd_im
                twisted[place, here, lanes] = (upper * c - lower * s).astype(jnp.bfloat16)
                twisted[place, below, lanes] = (upper * s + lower * c).astype(jnp.bfloat16)

    def finish(slot, place):
        mass = indices_ref[slot] % 64
        norm = jnp.sum(jnp.where(lane_id == mass, norm_row, 0.0), axis=1, keepdims=True)
        scale = lax.rsqrt(norm) * jnp.where(slot < count, 1.0, 0.0)
        for side in range(2):
            result = jnp.dot(
                last_ref[side],
                twisted[place, :, 256 * side : 256 * side + 256],
                preferred_element_type=jnp.float32,
            )
            scaled = result[: 2 * COLS] * scale
            for i in range(2):
                series[2 * side + i, pl.ds(slot, 2 * COLS, stride=TPL_DEV), :] = scaled[
                    :, 128 * i : 128 * i + 128
                ]

    @pl.loop(0, (count + BATCH - 1) // BATCH)
    def _(batch):
        for place in range(BATCH):
            multiply(batch * BATCH + place, place)
        for parity in range(2):
            middle[parity] = jnp.dot(
                products[parity], first_ref[parity], preferred_element_type=jnp.float32
            )
        for place in range(BATCH):
            twist(place)
        for place in range(BATCH):
            finish(batch * BATCH + place, place)

    def write(out_ref, half):
        for part in range(2):
            start = (part * COLS + 4 * half) * TPL_DEV
            for i in range(SPAN // 128):
                column, tile = divmod(i + 3, 4)
                rows = pl.ds(pl.multiple_of(start + column * TPL_DEV, TPL_DEV), TPL_DEV)
                out_ref[part, :, 128 * i : 128 * i + 128] = series[tile, rows, :].astype(
                    jnp.bfloat16
                )

    write(own_ref, half_ref[0])
    write(send_ref, 1 - half_ref[0])


def coherent_kernel(
    half_ref,
    delay_ref,
    near_gain_ref,
    far_gain_ref,
    own_ref,
    got_ref,
    out_ref,
    near,
    far,
    tiles,
    sems,
):
    def unpack(near_ref, far_ref):
        for part in range(2):
            near[part] = near_ref[part, :, 128 : 128 + HALF].astype(jnp.float32)
            far[part] = far_ref[part].astype(jnp.float32)[:, 64 : 64 + HALF + 128]

    @pl.when(half_ref[0] == 0)
    def _():
        unpack(own_ref, got_ref)

    @pl.when(half_ref[0] == 1)
    def _():
        unpack(got_ref, own_ref)

    lane_id = lax.broadcasted_iota(jnp.int32, (8, 128), 1)

    def copy_out(tile):
        lanes = pl.ds(pl.multiple_of(tile * 128, 128), 128)
        return pltpu.make_async_copy(tiles.at[tile], out_ref.at[:, lanes], sems.at[tile])

    @pl.loop(0, TILES // GROUP)
    def _(group):
        first_lane = pl.multiple_of(group * GROUP * 128, 128)
        for sky in range(SKY):
            shift = delay_ref[sky] + 64
            gain_near, gain_far = near_gain_ref[sky], far_gain_ref[sky]
            power = gain_near * gain_near + gain_far * gain_far
            inverse = lax.rsqrt(jnp.full((1, 128), power, jnp.float32))
            near_row = jnp.broadcast_to(gain_near * inverse, (8, 128))
            far_row = jnp.broadcast_to(gain_far * inverse, (8, 128))
            keep = lane_id < 128 - shift
            for upper in (0, 8):
                rows = slice(upper, upper + 8)
                total = [None] * GROUP
                for part in range(2):
                    rolled = [
                        pltpu.roll(far[part, rows, pl.ds(first_lane + 128 * i, 128)], 128 - shift, axis=1)
                        for i in range(GROUP + 1)
                    ]
                    for i in range(GROUP):
                        shifted = jnp.where(keep, rolled[i], rolled[i + 1])
                        own = near[part, rows, pl.ds(first_lane + 128 * i, 128)]
                        mixed = near_row * own + far_row * shifted
                        squared = mixed * mixed
                        total[i] = squared if part == 0 else total[i] + squared
                for i in range(GROUP):
                    place = pl.ds(sky + SKY * upper, 8, stride=SKY)
                    tiles[group * GROUP + i, place, :] = total[i]
        for i in range(GROUP):
            copy_out(group * GROUP + i).start()

    for tile in range(TILES):
        copy_out(tile).wait()


VMEM = pl.BlockSpec(memory_space=pltpu.VMEM)
SMEM = pl.BlockSpec(memory_space=pltpu.SMEM)


def on_device(strain, asd_inv, indices, counts, sky_delay, gain_near, gain_far):
    powers, first_tables, twist, last, scalars = constant_tables()
    z_groups, xy_groups = group_lists()
    bank = lax.axis_index("bank").astype(jnp.int32)[None]
    half = lax.axis_index("det").astype(jnp.int32)[None]
    payload = pl.pallas_call(
        prepare_kernel,
        out_shape=jax.ShapeDtypeStruct((N_Z, 1, PAYLOAD), jnp.float32),
        in_specs=[SMEM, VMEM, VMEM],
        out_specs=VMEM,
    )(bank, strain[0], asd_inv)
    line = lax.all_to_all(payload, "bank", 0, 0, axis_index_groups=z_groups)
    spread = pl.pallas_call(
        spread_kernel,
        out_shape=jax.ShapeDtypeStruct((N_XY, N_Z, PAYLOAD), jnp.bfloat16),
        in_specs=[VMEM],
        out_specs=VMEM,
    )(line)
    plane = lax.all_to_all(spread, "bank", 0, 0, axis_index_groups=xy_groups)
    waves = pl.pallas_call(
        wave_kernel,
        out_shape=jax.ShapeDtypeStruct((TPL_DEV, 2, DFT_COLS, 256), jnp.float32),
        in_specs=[SMEM] * 3 + [VMEM],
        out_specs=VMEM,
        cost_estimate=pl.CostEstimate(flops=40 * 2**20, bytes_accessed=10 * 2**20, transcendentals=2**20),
        compiler_params=pltpu.CompilerParams(vmem_limit_bytes=16 * 1024 * 1024),
    )(indices, counts, scalars, powers)
    window = jax.ShapeDtypeStruct((2, TPL_DEV, SPAN), jnp.bfloat16)
    own, send = pl.pallas_call(
        filter_kernel,
        out_shape=(window, window),
        in_specs=[SMEM] * 3 + [VMEM] * 5,
        out_specs=(VMEM, VMEM),
        scratch_shapes=[
            pltpu.VMEM((2, DFT_COLS, 256), jnp.float32),
            pltpu.VMEM((2, BATCH * DFT_COLS, 256), jnp.bfloat16),
            pltpu.VMEM((2, BATCH * DFT_COLS, 512), jnp.float32),
            pltpu.VMEM((BATCH, 512, 512), jnp.bfloat16),
            pltpu.VMEM((4, 2 * COLS * TPL_DEV, 128), jnp.float32),
        ],
        compiler_params=pltpu.CompilerParams(vmem_limit_bytes=24 * 1024 * 1024),
    )(indices, counts, half, waves, plane, first_tables, twist, last)
    got = lax.ppermute(send, "det", [(0, 1), (1, 0)])
    out = pl.pallas_call(
        coherent_kernel,
        out_shape=jax.ShapeDtypeStruct((TPL_DEV * SKY, HALF), jnp.float32),
        in_specs=[SMEM] * 4 + [VMEM] * 2,
        out_specs=pl.BlockSpec(memory_space=pl.ANY),
        scratch_shapes=[
            pltpu.VMEM((2, TPL_DEV, HALF), jnp.float32),
            pltpu.VMEM((2, TPL_DEV, HALF + 128), jnp.float32),
            pltpu.VMEM((TILES, TPL_DEV * SKY, 128), jnp.float32),
            pltpu.SemaphoreType.DMA((TILES,)),
        ],
        compiler_params=pltpu.CompilerParams(vmem_limit_bytes=16 * 1024 * 1024),
    )(half, sky_delay, gain_near, gain_far, own, got)
    return out.reshape(TPL_DEV, SKY, HALF)


def solution(mesh):
    return jax.shard_map(
        on_device,
        mesh=mesh,
        in_specs=(P("det", None, "bank"), P("det", "bank"), P("bank"), P("bank"), P(), P(), P()),
        out_specs=P("bank", None, "det"),
        check_vma=False,
    )
```

time: 75.9 us -> 63.7 us (0.84)
  the two profiles are of different devices: /device:TPU:129 before, /device:TPU:7 now
where the time goes in v2:
time: 63.7 us; the launch traced here: 63.3 us
  blocking collectives  20.9 us (33%)
  Pallas kernels  20 us (31%)
  starting transfers between devices  11.3 us (18%)
  local copies, waits for them, and re-layouts  9.26 us (15%)
  waiting for transfers between devices  0.99 us (2%)
  between operations  0.73 us (1%)
    all_to_all x1, blocking collectives, on_device(): line = lax.all_to_all(payload, 'bank', 0, 0, axis_index_groups=z_groups)  20.9 us
    unnamed x24, local copies, waits for them, and re-layouts  9.26 us
    all_to_all x1, starting transfers between devices, on_device(): plane = lax.all_to_all(spread, 'bank', 0, 0, axis_index_groups=xy_groups)  7.01 us
    pallas_call x1, Pallas kernels, on_device(): pl.pallas_call(filter_kernel, out_shape=(window, window), in_specs=[SMEM]...  6.98 us
    pallas_call x1, Pallas kernels, on_device(): pl.pallas_call(wave_kernel, out_shape=jax.ShapeDtypeStruct((TPL_DEV, 2, D...  6.48 us
    ppermute x1, starting transfers between devices, on_device(): got = lax.ppermute(send, 'det', [(0, 1), (1, 0)])  4.27 us
    pallas_call x1, Pallas kernels, on_device(): pl.pallas_call(coherent_kernel, out_shape=jax.ShapeDtypeStruct((TPL_DEV *...  3.52 us
    pallas_call x1, Pallas kernels, on_device(): pl.pallas_call(spread_kernel, out_shape=jax.ShapeDtypeStruct((N_XY, N_Z,...  1.55 us
  transfers between devices with their start and end apart: 2, of which 1 were waited for; matrix products, arithmetic and copies ran while one was open for 0% of the time, Pallas kernels for 10%

profile of v2, /device:TPU:7, one launch (start us, length us, event | category | flops | bytes accessed | tf_op | source)
XLA Modules:
  0.0 63.3 jit_solution(2165730505219155023)
XLA Ops:
  0.0 1.5 %shard_map.119 = f32[16,1,640]{2,1,0:T(1,128)} custom-call(s32[1]{0:T(128)} %bitcast.1.bank_ref, f32[2,256]{1,0:T(2,128)} %bitcast.4, f32[1,256]{1,0:T(1,128)} %asd_ref.1), custom_call_target="tpu_custom_call" | custom-call | tf_op jit(solution)/shard_map/pallas_call | solution.py:360
  1.5 20.9 %all_to_all.10.line_ref = f32[16,1,640]{2,1,0:T(1,128)} all-to-all(f32[16,1,640]{2,1,0:T(1,128)} %shard_map.119), channel_id=1, replica_groups={{16,20,24,28,0,4,8,12,18,22,26,30,2,6,10,14},{48,52,56,60,32,36,40,44,5..., dimensions={0} | all-to-all | bytes 81920 | tf_op jit(solution)/shard_map/all_to_all | solution.py:366
  22.4 1.6 %shard_map.120 = bf16[16,16,640]{2,1,0:T(8,128)(2,1)} custom-call(f32[16,1,640]{2,1,0:T(1,128)} %all_to_all.10.line_ref), custom_call_target="tpu_custom_call" | custom-call | tf_op jit(solution)/shard_map/pallas_call | solution.py:367
  24.0 7.0 %all-to-all-start.1 = ((bf16[16,16,640]{2,1,0:T(8,128)(2,1)}), bf16[16,16,640]{2,1,0:T(8,128)(2,1)S(1)}, u32[]{:S(2)}, u32[]{:S(2)}) async-start(bf16[16,16,640]{2,1,0:T(8,128)(2,1)} %shard_map.120), calls=%async_computation.1 | async-start | bytes 655360 | tf_op jit(solution)/shard_map/all_to_all | solution.py:373
  31.7 0.0 copy-start.2
  31.7 1.3 %copy-done.2 = f32[5,256,256]{2,1,0:T(8,128)S(1)} copy-done((f32[5,256,256]{2,1,0:T(8,128)S(1)}, f32[5,256,256]{2,1,0:T(8,128)}, u32[]{:S(2)}) %copy-start.2) | copy-done | bytes 1310744
  33.0 0.0 copy-start.6
  33.0 0.7 %copy-done.6 = f32[8,64]{1,0:T(8,128)S(1)} copy-done((f32[8,64]{1,0:T(8,128)S(1)}, f32[8,64]{1,0:T(8,128)}, u32[]{:S(2)}) %copy-start.6) | copy-done | bytes 2072
  33.7 0.0 copy-start.7
  33.7 0.7 %copy-done.7 = s32[16]{0:T(128)S(1)} copy-done((s32[16]{0:T(128)S(1)}, s32[16]{0:T(128)}, u32[]{:S(2)}) %copy-start.7) | copy-done | bytes 88
  34.3 0.0 copy-start.3
  34.3 0.0 copy-start.4
  34.3 0.0 copy-start.5
  34.3 0.0 copy-start.8
  34.3 6.5 %shard_map.118.waves_ref = f32[16,2,256,256]{3,2,1,0:T(8,128)S(1)} custom-call(s32[16]{0:T(128)S(1)} %copy-done.7, s32[1]{0:T(128)S(6)} %copy.13.counts_ref, f32[8,64]{1,0:T(8,128)S(1)} %copy-done.6, f32[5,256,256]{2,1,0:T(8,128)S(1)} %copy-done.2), custom_call_target="tpu_custom_call" | custom-call | flops 41943040 | bytes 10485760 | tf_op jit(solution)/shard_map/pallas_call | solution.py:374
  40.8 0.0 copy-start
  40.8 3.2 %copy-done = f32[16,2,256,256]{3,2,1,0:T(8,128)} copy-done((f32[16,2,256,256]{3,2,1,0:T(8,128)}, f32[16,2,256,256]{3,2,1,0:T(8,128)S(1)}, u32[]{:S(2)}) %copy-start) | copy-done | bytes 8388632
  44.0 0.0 all-to-all-done.1.gathered_ref
  44.0 0.0 copy-done.3
  44.0 0.0 copy-done.4
  44.1 0.0 copy-done.5
  44.1 0.0 copy-done.8
  44.1 0.0 copy-start.1
  44.1 3.4 %copy-done.1 = f32[16,2,256,256]{3,2,1,0:T(8,128)S(1)} copy-done((f32[16,2,256,256]{3,2,1,0:T(8,128)S(1)}, f32[16,2,256,256]{3,2,1,0:T(8,128)}, u32[]{:S(2)}) %copy-start.1) | copy-done | bytes 8388632
  47.5 0.0 copy-start.9
  47.5 7.0 %shard_map.121 = (bf16[2,16,2304]{2,1,0:T(8,128)(2,1)S(1)}, bf16[2,16,2304]{2,1,0:T(8,128)(2,1)S(1)}) custom-call(s32[16]{0:T(128)S(1)} %copy-done.8, s32[1]{0:T(128)S(6)} %copy.13.counts_ref, s32[1]{0:T(128)} %bitcast.half_ref, f32[16,2,256,256]{3,2,1,0:T(8,128)S(1)} %copy-done.1, bf16[16,16,640]{2,1,0:T(8,128)(2,1)S(1)} %all-to-all-done.1.gathered_ref, ...), custom_call_target="tpu_custom_call" | custom-call | tf_op jit(solution)/shard_map/pallas_call | solution.py:383
  54.5 4.3 %collective-permute-start = (bf16[2,16,2304]{2,1,0:T(8,128)(2,1)S(1)}, bf16[2,16,2304]{2,1,0:T(8,128)(2,1)S(1)}, u32[]{:S(2)}, u32[]{:S(2)}) collective-permute-start(bf16[2,16,2304]{2,1,0:T(8,128)(2,1)S(1)} %get-tuple-element.8), channel_id=1, source_target_pairs={{0,1},{1,0},{2,3},{3,2},{4,5},{5,4},{6,7},{7,6},{8,9},{9,8},{10,11... | collective-permute-start | bytes 442376 | tf_op jit(solution)/shard_map/ppermute | solution.py:397
  58.7 1.0 %collective-permute-done.got_ref = bf16[2,16,2304]{2,1,0:T(8,128)(2,1)S(1)} collective-permute-done((bf16[2,16,2304]{2,1,0:T(8,128)(2,1)S(1)}, bf16[2,16,2304]{2,1,0:T(8,128)(2,1)S(1)}, u32[]{:S(2)}, u32[]{:S(2)}) %collective-permute-start) | collective-permute-done | bytes 147488 | tf_op jit(solution)/shard_map/ppermute | solution.py:397
  59.7 0.0 copy-done.9
  59.7 0.0 copy-done.10
  59.7 0.0 copy-done.11
  59.7 3.5 %shard_map.122 = f32[256,2048]{1,0:T(8,128)} custom-call(s32[1]{0:T(128)} %bitcast.half_ref, s32[16]{0:T(128)S(1)} %copy-done.9, f32[16]{0:T(128)S(1)} %copy-done.10, f32[16]{0:T(128)S(1)} %copy-done.11, bf16[2,16,2304]{2,1,0:T(8,128)(2,1)S(1)} %get-tuple-element.7.own_ref, bf16[2,16,2304]{2,1,0:T(8,128)(2,1)S(1)} %collective-permute-done.got_ref), custom_call_target="tpu_custom_call" | custom-call | tf_op jit(solution)/shard_map/pallas_call | solution.py:398
  (2 shorter events, 0.0 us)
Async XLA Ops:
  24.0 20.0 %all-to-all-start.1 = ((bf16[16,16,640]{2,1,0:T(8,128)(2,1)}), bf16[16,16,640]{2,1,0:T(8,128)(2,1)S(1)}, u32[]{:S(2)}, u32[]{:S(2)}) async-start(bf16[16,16,640]{2,1,0:T(8,128)(2,1)} %shard_map.120), calls=%async_computation.1 | async-start | bytes 655360 | tf_op jit(solution)/shard_map/all_to_all | solution.py:373
  31.7 1.3 %copy-start.2 = (f32[5,256,256]{2,1,0:T(8,128)S(1)}, f32[5,256,256]{2,1,0:T(8,128)}, u32[]{:S(2)}) copy-start(f32[5,256,256]{2,1,0:T(8,128)} %constant.19.clone.powers_ref) | copy-start | bytes 3932164
  33.0 0.7 %copy-start.6 = (f32[8,64]{1,0:T(8,128)S(1)}, f32[8,64]{1,0:T(8,128)}, u32[]{:S(2)}) copy-start(f32[8,64]{1,0:T(8,128)} %constant.18.clone.scalars_ref) | copy-start | bytes 6148
  33.7 0.7 %copy-start.7 = (s32[16]{0:T(128)S(1)}, s32[16]{0:T(128)}, u32[]{:S(2)}) copy-start(s32[16]{0:T(128)} %indices_ref.3) | copy-start | bytes 196
  34.3 9.7 %copy-start.3 = (f32[2,256,256]{2,1,0:T(8,128)S(1)}, f32[2,256,256]{2,1,0:T(8,128)}, u32[]{:S(2)}) copy-start(f32[2,256,256]{2,1,0:T(8,128)} %constant.21.clone.twist_ref) | copy-start | bytes 1572868
  34.3 9.7 %copy-start.4 = (bf16[2,256,512]{2,1,0:T(8,128)(2,1)S(1)}, bf16[2,256,512]{2,1,0:T(8,128)(2,1)}, u32[]{:S(2)}) copy-start(bf16[2,256,512]{2,1,0:T(8,128)(2,1)} %constant.20.clone.first_ref) | copy-start | bytes 1572868
  34.3 9.7 %copy-start.5 = (bf16[2,32,512]{2,1,0:T(8,128)(2,1)S(1)}, bf16[2,32,512]{2,1,0:T(8,128)(2,1)}, u32[]{:S(2)}) copy-start(bf16[2,32,512]{2,1,0:T(8,128)(2,1)} %constant.22.clone.last_ref) | copy-start | bytes 196612
  34.3 9.7 %copy-start.8 = (s32[16]{0:T(128)S(1)}, s32[16]{0:T(128)}, u32[]{:S(2)}) copy-start(s32[16]{0:T(128)} %indices_ref.3) | copy-start | bytes 196
  40.8 3.2 %copy-start = (f32[16,2,256,256]{3,2,1,0:T(8,128)}, f32[16,2,256,256]{3,2,1,0:T(8,128)S(1)}, u32[]{:S(2)}) copy-start(f32[16,2,256,256]{3,2,1,0:T(8,128)S(1)} %shard_map.118.waves_ref) | copy-start | bytes 25165828
  44.1 3.4 %copy-start.1 = (f32[16,2,256,256]{3,2,1,0:T(8,128)S(1)}, f32[16,2,256,256]{3,2,1,0:T(8,128)}, u32[]{:S(2)}) copy-start(f32[16,2,256,256]{3,2,1,0:T(8,128)} %copy-done) | copy-start | bytes 25165828
  47.5 12.3 %copy-start.9 = (s32[16]{0:T(128)S(1)}, s32[16]{0:T(128)}, u32[]{:S(2)}) copy-start(s32[16]{0:T(128)} %delay_ref.1) | copy-start | bytes 196
  47.5 12.3 %copy-start.10 = (f32[16]{0:T(128)S(1)}, f32[16]{0:T(128)}, u32[]{:S(2)}) copy-start(f32[16]{0:T(128)} %near_gain_ref.1) | copy-start | bytes 196
  47.5 12.3 %copy-start.11 = (f32[16]{0:T(128)S(1)}, f32[16]{0:T(128)}, u32[]{:S(2)}) copy-start(f32[16]{0:T(128)} %far_gain_ref.1) | copy-start | bytes 196
  54.5 5.3 %collective-permute-start = (bf16[2,16,2304]{2,1,0:T(8,128)(2,1)S(1)}, bf16[2,16,2304]{2,1,0:T(8,128)(2,1)S(1)}, u32[]{:S(2)}, u32[]{:S(2)}) collective-permute-start(bf16[2,16,2304]{2,1,0:T(8,128)(2,1)S(1)} %get-tuple-element.8), channel_id=1, source_target_pairs={{0,1},{1,0},{2,3},{3,2},{4,5},{5,4},{6,7},{7,6},{8,9},{9,8},{10,11... | collective-permute-start | bytes 442376 | tf_op jit(solution)/shard_map/ppermute | solution.py:397

commit v3 on v2

--- a/solution.py
+++ b/solution.py
@@ -1,3 +1,4 @@
+import functools
 import math
 
 import jax
@@ -25,8 +26,13 @@
 PAYLOAD = 640
 STRIP = 16
 BATCH = 4
+STORED = 3
 TILES = HALF // 128
 GROUP = 4
+STAGES = 4
+BIG = 60 * 1024 * 1024
+FILTER_VMEM = 46 * 1024 * 1024
+WAVE_ROOM = 80
 
 MSUN_SEC = 4.925491e-06
 SAMPLE_RATE = 2048.0
@@ -122,27 +128,101 @@
     return total
 
 
-def prepare_kernel(bank_ref, strain_ref, asd_ref, out_ref):
-    weight = asd_ref[...] * asd_ref[...]
-    over = strain_ref[...] * weight
-    bin_id = bank_ref[0] * 256 + lax.broadcasted_iota(jnp.int32, (1, 256), 1)
+def payload_row(bank, strain, asd):
+    weight = asd * asd
+    over = (strain * weight).astype(jnp.bfloat16).astype(jnp.float32)
+    bin_id = bank * 256 + lax.broadcasted_iota(jnp.int32, (1, 256), 1)
     clipped = jnp.maximum(bin_id.astype(jnp.float32) * (SAMPLE_RATE / SAMPLES), 1.0)
     square = clipped * clipped
-    weighted = jnp.where(
-        bin_id >= LOW_BIN, jnp.exp((-7.0 / 3.0) * jnp.log(clipped)), 0.0
-    ) * weight
+    falling = jnp.exp((-7.0 / 3.0) * jnp.log(clipped))
+    weighted = jnp.where(bin_id >= LOW_BIN, falling, 0.0) * weight
     mass_id = lax.broadcasted_iota(jnp.int32, (MASSES, 1), 0).astype(jnp.float32)
     start = math.log(2.0) + 4.0 * math.log(6.0**1.5 * math.pi * 6.0 * MSUN_SEC)
     steep = jnp.exp(4.0 * math.log(1.03) * mass_id + start)
-    terms = jnp.exp(-steep * (square * square)) * weighted
-    column = jnp.sum(terms, axis=1, keepdims=True)
+    column = jnp.sum(jnp.exp(-steep * (square * square)) * weighted, axis=1, keepdims=True)
     row_id = lax.broadcasted_iota(jnp.int32, (MASSES, MASSES), 0)
     col_id = lax.broadcasted_iota(jnp.int32, (MASSES, MASSES), 1)
     norms = jnp.sum(jnp.where(row_id == col_id, column, 0.0), axis=0, keepdims=True)
     coarse = norms.astype(jnp.bfloat16).astype(jnp.float32)
-    row = jnp.concatenate(
-        [over[0:1].astype(jnp.bfloat16).astype(jnp.float32), over[1:2].astype(jnp.bfloat16).astype(jnp.float32), coarse, norms - coarse], axis=1
+    return jnp.concatenate([over[0:1], over[1:2], coarse, norms - coarse], axis=1)
+
+
+def slot_scalars(slot, indices_ref, scalars_ref):
+    entry = indices_ref[slot]
+    mass, eta = entry % 64, entry // 64 % 64
+    spin = -0.6 + 0.4 * (entry // 4096).astype(jnp.float32)
+    lead = scalars_ref[4, eta]
+    c53 = lead * scalars_ref[0, mass]
+    c1 = lead * scalars_ref[5, eta] * scalars_ref[1, mass]
+    c23 = lead * (4.0 * spin * scalars_ref[6, eta] - 16.0 * math.pi) * scalars_ref[2, mass]
+    return c53, c1, c23, scalars_ref[3, mass]
+
+
+def wave(coefs, powers, here):
+    c53, c1, c23, steep = coefs
+    turns = (
+        c53 * powers[0, here, :] + c1 * powers[1, here, :] + (c23 * powers[2, here, :] - 0.125)
     )
+    rest = turns - ((turns + ROUND_SHIFT) - ROUND_SHIFT)
+    square = rest * rest
+    half_sin = horner(SIN_FIT, square) * rest
+    half_cos = horner(COS_FIT, square)
+    envelope = powers[3, here, :] * jnp.exp2(steep * powers[4, here, :])
+    return envelope * (1.0 - half_sin * half_sin), envelope * (half_sin * half_cos)
+
+
+def wave_kernel(indices_ref, counts_ref, scalars_ref, powers_hbm, waves_ref, powers, staged, sems):
+    steps = rounded_up(counts_ref[0]) // BATCH * STORED
+
+    def store(step):
+        place = step % STAGES
+        return pltpu.make_async_copy(staged.at[place], waves_ref.at[step], sems.at[place])
+
+    def load(strip):
+        rows = pl.ds(strip * 64, 64)
+        return pltpu.make_async_copy(
+            powers_hbm.at[:, rows], powers.at[:, rows], sems.at[STAGES + strip]
+        )
+
+    for strip in range(4):
+        load(strip).start()
+
+    @pl.loop(0, steps)
+    def _(step):
+        slot = step // STORED * BATCH + step % STORED
+        coefs = slot_scalars(slot, indices_ref, scalars_ref)
+
+        @pl.when(step >= STAGES)
+        def _():
+            store(step - STAGES).wait()
+
+        @pl.loop(0, DFT_COLS // 64)
+        def _(strip):
+            @pl.when(step == 0)
+            def _():
+                load(strip).wait()
+
+            for piece in range(4):
+                here = pl.ds(pl.multiple_of(strip * 64 + piece * 16, 16), 16)
+                cosine, sine = wave(coefs, powers, here)
+                staged[step % STAGES, 0, here, :] = cosine.astype(jnp.bfloat16)
+                staged[step % STAGES, 1, here, :] = sine.astype(jnp.bfloat16)
+
+        store(step).start()
+
+    for back in range(STAGES, 0, -1):
+
+        @pl.when(steps >= back)
+        def _():
+            store(steps - back).wait()
+
+
+def rounded_up(count):
+    return (count + BATCH - 1) // BATCH * BATCH
+
+
+def prepare_kernel(bank_ref, strain_ref, asd_ref, out_ref):
+    row = payload_row(bank_ref[0], strain_ref[...], asd_ref[...])
     out_ref[...] = jnp.broadcast_to(row[:, None, :], (N_Z, 1, PAYLOAD))
 
 
@@ -152,45 +232,17 @@
         out_ref[i] = line
 
 
-def wave_kernel(indices_ref, counts_ref, scalars_ref, powers_ref, waves_ref):
-    @pl.loop(0, (counts_ref[0] + BATCH - 1) // BATCH * BATCH)
-    def _(slot):
-        entry = indices_ref[slot]
-        mass, eta = entry % 64, entry // 64 % 64
-        spin = -0.6 + 0.4 * (entry // 4096).astype(jnp.float32)
-        lead = scalars_ref[4, eta]
-        c53 = lead * scalars_ref[0, mass]
-        c1 = lead * scalars_ref[5, eta] * scalars_ref[1, mass]
-        c23 = lead * (4.0 * spin * scalars_ref[6, eta] - 16.0 * math.pi) * scalars_ref[2, mass]
-        steep = scalars_ref[3, mass]
-
-        @pl.loop(0, DFT_COLS // 64)
-        def _(strip):
-            for step in range(8):
-                here = pl.ds(pl.multiple_of(strip * 64 + step * 8, 8), 8)
-                turns = (
-                    c53 * powers_ref[0, here, :]
-                    + c1 * powers_ref[1, here, :]
-                    + (c23 * powers_ref[2, here, :] - 0.125)
-                )
-                rest = turns - ((turns + ROUND_SHIFT) - ROUND_SHIFT)
-                square = rest * rest
-                half_sin = horner(SIN_FIT, square) * rest
-                half_cos = horner(COS_FIT, square)
-                envelope = powers_ref[3, here, :] * jnp.exp2(steep * powers_ref[4, here, :])
-                waves_ref[slot, 0, here, :] = envelope * (1.0 - half_sin * half_sin)
-                waves_ref[slot, 1, here, :] = envelope * (half_sin * half_cos)
-
-
 def filter_kernel(
     indices_ref,
     counts_ref,
     half_ref,
-    waves_ref,
+    scalars_ref,
     gathered_ref,
     first_ref,
     twist_ref,
     last_ref,
+    powers_ref,
+    waves_ref,
     own_ref,
     send_ref,
     spectrum,
@@ -198,8 +250,21 @@
     middle,
     twisted,
     series,
+    waves,
+    sems,
 ):
     count = counts_ref[0]
+    batches = rounded_up(count) // BATCH
+    steps = batches * STORED
+
+    def fetch(step):
+        place = step % (2 * STORED)
+        return pltpu.make_async_copy(waves_ref.at[step], waves.at[place], sems.at[place])
+
+    @pl.loop(0, jnp.minimum(steps, 2 * STORED))
+    def _(step):
+        fetch(step).start()
+
     for part in range(2):
         block = gathered_ref[:, :, 256 * part : 256 * part + 256].astype(jnp.float32)
         for parity in range(2):
@@ -212,10 +277,20 @@
     lane_id = lax.broadcasted_iota(jnp.int32, (1, MASSES), 1)
     series[...] = jnp.zeros_like(series)
 
-    def multiply(slot, place):
+    def multiply(batch, place):
+        if place < STORED:
+            step = batch * STORED + place
+            buffer = step % (2 * STORED)
+            fetch(step).wait()
+        else:
+            coefs = slot_scalars(batch * BATCH + place, indices_ref, scalars_ref)
         for i in range(0, DFT_COLS, STRIP):
             here, there = slice(i, i + STRIP), slice(256 * place + i, 256 * place + i + STRIP)
-            cosine, sine = waves_ref[slot, 0, here, :], waves_ref[slot, 1, here, :]
+            if place < STORED:
+                cosine = waves[buffer, 0, here, :].astype(jnp.float32)
+                sine = waves[buffer, 1, here, :].astype(jnp.float32)
+            else:
+                cosine, sine = wave(coefs, powers_ref, here)
             re, im = spectrum[0, here, :], spectrum[1, here, :]
             real_part = (re * cosine - im * sine).astype(jnp.bfloat16)
             imag_part = (re * sine + im * cosine).astype(jnp.bfloat16)
@@ -254,10 +329,18 @@
                     :, 128 * i : 128 * i + 128
                 ]
 
-    @pl.loop(0, (count + BATCH - 1) // BATCH)
+    @pl.loop(0, batches)
     def _(batch):
         for place in range(BATCH):
-            multiply(batch * BATCH + place, place)
+            multiply(batch, place)
+
+        for place in range(STORED):
+            later = (batch + 2) * STORED + place
+
+            @pl.when(later < steps)
+            def _():
+                fetch(later).start()
+
         for parity in range(2):
             middle[parity] = jnp.dot(
                 products[parity], first_ref[parity], preferred_element_type=jnp.float32
@@ -348,6 +431,7 @@
         copy_out(tile).wait()
 
 
+ANY = pl.BlockSpec(memory_space=pl.ANY)
 VMEM = pl.BlockSpec(memory_space=pltpu.VMEM)
 SMEM = pl.BlockSpec(memory_space=pltpu.SMEM)
 
@@ -362,6 +446,7 @@
         out_shape=jax.ShapeDtypeStruct((N_Z, 1, PAYLOAD), jnp.float32),
         in_specs=[SMEM, VMEM, VMEM],
         out_specs=VMEM,
+        compiler_params=pltpu.CompilerParams(vmem_limit_bytes=BIG),
     )(bank, strain[0], asd_inv)
     line = lax.all_to_all(payload, "bank", 0, 0, axis_index_groups=z_groups)
     spread = pl.pallas_call(
@@ -373,17 +458,24 @@
     plane = lax.all_to_all(spread, "bank", 0, 0, axis_index_groups=xy_groups)
     waves = pl.pallas_call(
         wave_kernel,
-        out_shape=jax.ShapeDtypeStruct((TPL_DEV, 2, DFT_COLS, 256), jnp.float32),
-        in_specs=[SMEM] * 3 + [VMEM],
-        out_specs=VMEM,
-        cost_estimate=pl.CostEstimate(flops=40 * 2**20, bytes_accessed=10 * 2**20, transcendentals=2**20),
-        compiler_params=pltpu.CompilerParams(vmem_limit_bytes=16 * 1024 * 1024),
+        out_shape=jax.ShapeDtypeStruct((WAVE_ROOM, 2, DFT_COLS, 256), jnp.bfloat16),
+        in_specs=[SMEM] * 3 + [ANY],
+        out_specs=ANY,
+        scratch_shapes=[
+            pltpu.VMEM((5, DFT_COLS, 256), jnp.float32),
+            pltpu.VMEM((STAGES, 2, DFT_COLS, 256), jnp.bfloat16),
+            pltpu.SemaphoreType.DMA((STAGES + 4,)),
+        ],
+        cost_estimate=pl.CostEstimate(
+            flops=40 * 2**20, bytes_accessed=10 * 2**20, transcendentals=2**20
+        ),
+        compiler_params=pltpu.CompilerParams(vmem_limit_bytes=BIG),
     )(indices, counts, scalars, powers)
     window = jax.ShapeDtypeStruct((2, TPL_DEV, SPAN), jnp.bfloat16)
     own, send = pl.pallas_call(
         filter_kernel,
         out_shape=(window, window),
-        in_specs=[SMEM] * 3 + [VMEM] * 5,
+        in_specs=[SMEM] * 4 + [VMEM] * 5 + [ANY],
         out_specs=(VMEM, VMEM),
         scratch_shapes=[
             pltpu.VMEM((2, DFT_COLS, 256), jnp.float32),
@@ -391,9 +483,11 @@
             pltpu.VMEM((2, BATCH * DFT_COLS, 512), jnp.float32),
             pltpu.VMEM((BATCH, 512, 512), jnp.bfloat16),
             pltpu.VMEM((4, 2 * COLS * TPL_DEV, 128), jnp.float32),
+            pltpu.VMEM((2 * STORED, 2, DFT_COLS, 256), jnp.bfloat16),
+            pltpu.SemaphoreType.DMA((2 * STORED,)),
         ],
-        compiler_params=pltpu.CompilerParams(vmem_limit_bytes=24 * 1024 * 1024),
-    )(indices, counts, half, waves, plane, first_tables, twist, last)
+        compiler_params=pltpu.CompilerParams(vmem_limit_bytes=FILTER_VMEM),
+    )(indices, counts, half, scalars, plane, first_tables, twist, last, powers, waves)
     got = lax.ppermute(send, "det", [(0, 1), (1, 0)])
     out = pl.pallas_call(
         coherent_kernel,

time: 63.7 us -> 56 us (0.88)
  the two profiles are of different devices: /device:TPU:7 before, /device:TPU:69 now
where the time goes in v3:
time: 56 us; the launch traced here: 55.5 us
  Pallas kernels  23.3 us (42%)
  blocking collectives  20 us (36%)
  starting transfers between devices  10.4 us (19%)
  waiting for transfers between devices  0.99 us (2%)
  between operations  0.81 us (1%)
    all_to_all x1, blocking collectives, on_device(): line = lax.all_to_all(payload, 'bank', 0, 0, axis_index_groups=z_groups)  20 us
    pallas_call x1, Pallas kernels, on_device(): pl.pallas_call(filter_kernel, out_shape=(window, window), in_specs=[SMEM]...  9.37 us
    pallas_call x1, Pallas kernels, on_device(): pl.pallas_call(wave_kernel, out_shape=jax.ShapeDtypeStruct((WAVE_ROOM, 2,...  7.31 us
    all_to_all x1, starting transfers between devices, on_device(): plane = lax.all_to_all(spread, 'bank', 0, 0, axis_index_groups=xy_groups)  6.13 us
    ppermute x1, starting transfers between devices, on_device(): got = lax.ppermute(send, 'det', [(0, 1), (1, 0)])  4.25 us
    pallas_call x1, Pallas kernels, on_device(): pl.pallas_call(coherent_kernel, out_shape=jax.ShapeDtypeStruct((TPL_DEV *...  3.52 us
    pallas_call x1, Pallas kernels, on_device(): pl.pallas_call(spread_kernel, out_shape=jax.ShapeDtypeStruct((N_XY, N_Z,...  1.55 us
    pallas_call x1, Pallas kernels, on_device(): pl.pallas_call(prepare_kernel, out_shape=jax.ShapeDtypeStruct((N_Z, 1, PA...  1.51 us
  transfers between devices with their start and end apart: 2, of which 1 were waited for; matrix products, arithmetic and copies ran while one was open for 0% of the time, Pallas kernels for 13%

profile of v3, /device:TPU:69, one launch (start us, length us, event | category | flops | bytes accessed | tf_op | source)
XLA Modules:
  0.0 55.5 jit_solution(7334227969666506453)
XLA Ops:
  0.0 1.5 %shard_map.118 = f32[16,1,640]{2,1,0:T(1,128)} custom-call(s32[1]{0:T(128)} %bitcast.1.bank_ref, f32[2,256]{1,0:T(2,128)} %bitcast.4, f32[1,256]{1,0:T(1,128)} %asd_ref.1), custom_call_target="tpu_custom_call" | custom-call | tf_op jit(solution)/shard_map/pallas_call | solution.py:444
  1.5 20.0 %all_to_all.10.line_ref = f32[16,1,640]{2,1,0:T(1,128)} all-to-all(f32[16,1,640]{2,1,0:T(1,128)} %shard_map.118), channel_id=1, replica_groups={{16,20,24,28,0,4,8,12,18,22,26,30,2,6,10,14},{48,52,56,60,32,36,40,44,5..., dimensions={0} | all-to-all | bytes 81920 | tf_op jit(solution)/shard_map/all_to_all | solution.py:451
  21.5 1.6 %shard_map.119 = bf16[16,16,640]{2,1,0:T(8,128)(2,1)} custom-call(f32[16,1,640]{2,1,0:T(1,128)} %all_to_all.10.line_ref), custom_call_target="tpu_custom_call" | custom-call | tf_op jit(solution)/shard_map/pallas_call | solution.py:452
  23.1 6.1 %all-to-all-start.1 = ((bf16[16,16,640]{2,1,0:T(8,128)(2,1)}), bf16[16,16,640]{2,1,0:T(8,128)(2,1)S(1)}, u32[]{:S(2)}, u32[]{:S(2)}) async-start(bf16[16,16,640]{2,1,0:T(8,128)(2,1)} %shard_map.119), calls=%async_computation.1 | async-start | bytes 655360 | tf_op jit(solution)/shard_map/all_to_all | solution.py:458
  29.9 0.0 copy-start
  29.9 0.0 copy-start.1
  29.9 0.0 copy-start.2
  29.9 0.0 copy-start.3
  29.9 0.0 copy-start.4
  29.9 0.0 copy-start.5
  30.0 7.3 %shard_map.120.waves_ref = bf16[80,2,256,256]{3,2,1,0:T(8,128)(2,1)} custom-call(s32[16]{0:T(128)} %indices_ref.3, s32[1]{0:T(128)S(6)} %copy.13.counts_ref, f32[8,64]{1,0:T(8,128)} %constant.18.clone.scalars_ref, f32[5,256,256]{2,1,0:T(8,128)} %constant.19.clone.powers_hbm.powers_ref), custom_call_target="tpu_custom_call" | custom-call | flops 41943040 | bytes 10485760 | tf_op jit(solution)/shard_map/pallas_call | solution.py:459
  37.3 0.0 all-to-all-done.1.gathered_ref
  37.3 0.0 copy-done
  37.3 0.0 copy-done.1
  37.3 0.0 copy-done.2
  37.3 0.0 copy-done.3
  37.3 0.0 copy-done.4
  37.3 0.0 copy-done.5
  37.3 0.0 copy-start.6
  37.4 0.0 copy-start.7
  37.4 0.0 copy-start.8
  37.4 9.4 %shard_map.121 = (bf16[2,16,2304]{2,1,0:T(8,128)(2,1)S(1)}, bf16[2,16,2304]{2,1,0:T(8,128)(2,1)S(1)}) custom-call(s32[16]{0:T(128)S(1)} %copy-done.5, s32[1]{0:T(128)S(6)} %copy.13.counts_ref, s32[1]{0:T(128)} %bitcast.half_ref, f32[8,64]{1,0:T(8,128)S(1)} %copy-done.4, bf16[16,16,640]{2,1,0:T(8,128)(2,1)S(1)} %all-to-all-done.1.gathered_ref, ...), custom_call_target="tpu_custom_call" | custom-call | tf_op jit(solution)/shard_map/pallas_call | solution.py:475
  46.8 4.3 %collective-permute-start = (bf16[2,16,2304]{2,1,0:T(8,128)(2,1)S(1)}, bf16[2,16,2304]{2,1,0:T(8,128)(2,1)S(1)}, u32[]{:S(2)}, u32[]{:S(2)}) collective-permute-start(bf16[2,16,2304]{2,1,0:T(8,128)(2,1)S(1)} %get-tuple-element.8), channel_id=1, source_target_pairs={{0,1},{1,0},{2,3},{3,2},{4,5},{5,4},{6,7},{7,6},{8,9},{9,8},{10,11... | collective-permute-start | bytes 442376 | tf_op jit(solution)/shard_map/ppermute | solution.py:491
  51.0 1.0 %collective-permute-done.got_ref = bf16[2,16,2304]{2,1,0:T(8,128)(2,1)S(1)} collective-permute-done((bf16[2,16,2304]{2,1,0:T(8,128)(2,1)S(1)}, bf16[2,16,2304]{2,1,0:T(8,128)(2,1)S(1)}, u32[]{:S(2)}, u32[]{:S(2)}) %collective-permute-start) | collective-permute-done | bytes 147488 | tf_op jit(solution)/shard_map/ppermute | solution.py:491
  52.0 0.0 copy-done.6
  52.0 0.0 copy-done.7
  52.0 0.0 copy-done.8
  52.0 3.5 %shard_map.122 = f32[256,2048]{1,0:T(8,128)} custom-call(s32[1]{0:T(128)} %bitcast.half_ref, s32[16]{0:T(128)S(1)} %copy-done.6, f32[16]{0:T(128)S(1)} %copy-done.7, f32[16]{0:T(128)S(1)} %copy-done.8, bf16[2,16,2304]{2,1,0:T(8,128)(2,1)S(1)} %get-tuple-element.7.own_ref, bf16[2,16,2304]{2,1,0:T(8,128)(2,1)S(1)} %collective-permute-done.got_ref), custom_call_target="tpu_custom_call" | custom-call | tf_op jit(solution)/shard_map/pallas_call | solution.py:492
Async XLA Ops:
  23.1 14.2 %all-to-all-start.1 = ((bf16[16,16,640]{2,1,0:T(8,128)(2,1)}), bf16[16,16,640]{2,1,0:T(8,128)(2,1)S(1)}, u32[]{:S(2)}, u32[]{:S(2)}) async-start(bf16[16,16,640]{2,1,0:T(8,128)(2,1)} %shard_map.119), calls=%async_computation.1 | async-start | bytes 655360 | tf_op jit(solution)/shard_map/all_to_all | solution.py:458
  29.9 7.4 %copy-start = (f32[5,256,256]{2,1,0:T(8,128)S(1)}, f32[5,256,256]{2,1,0:T(8,128)}, u32[]{:S(2)}) copy-start(f32[5,256,256]{2,1,0:T(8,128)} %constant.19.clone.powers_hbm.powers_ref) | copy-start | bytes 3932164
  29.9 7.4 %copy-start.1 = (f32[2,256,256]{2,1,0:T(8,128)S(1)}, f32[2,256,256]{2,1,0:T(8,128)}, u32[]{:S(2)}) copy-start(f32[2,256,256]{2,1,0:T(8,128)} %constant.21.clone.twist_ref) | copy-start | bytes 1572868
  29.9 7.4 %copy-start.2 = (bf16[2,256,512]{2,1,0:T(8,128)(2,1)S(1)}, bf16[2,256,512]{2,1,0:T(8,128)(2,1)}, u32[]{:S(2)}) copy-start(bf16[2,256,512]{2,1,0:T(8,128)(2,1)} %constant.20.clone.first_ref) | copy-start | bytes 1572868
  29.9 7.4 %copy-start.3 = (bf16[2,32,512]{2,1,0:T(8,128)(2,1)S(1)}, bf16[2,32,512]{2,1,0:T(8,128)(2,1)}, u32[]{:S(2)}) copy-start(bf16[2,32,512]{2,1,0:T(8,128)(2,1)} %constant.22.clone.last_ref) | copy-start | bytes 196612
  29.9 7.4 %copy-start.4 = (f32[8,64]{1,0:T(8,128)S(1)}, f32[8,64]{1,0:T(8,128)}, u32[]{:S(2)}) copy-start(f32[8,64]{1,0:T(8,128)} %constant.18.clone.scalars_ref) | copy-start | bytes 6148
  29.9 7.4 %copy-start.5 = (s32[16]{0:T(128)S(1)}, s32[16]{0:T(128)}, u32[]{:S(2)}) copy-start(s32[16]{0:T(128)} %indices_ref.3) | copy-start | bytes 196
  37.3 14.7 %copy-start.6 = (s32[16]{0:T(128)S(1)}, s32[16]{0:T(128)}, u32[]{:S(2)}) copy-start(s32[16]{0:T(128)} %delay_ref.1) | copy-start | bytes 196
  37.4 14.7 %copy-start.7 = (f32[16]{0:T(128)S(1)}, f32[16]{0:T(128)}, u32[]{:S(2)}) copy-start(f32[16]{0:T(128)} %near_gain_ref.1) | copy-start | bytes 196
  37.4 14.6 %copy-start.8 = (f32[16]{0:T(128)S(1)}, f32[16]{0:T(128)}, u32[]{:S(2)}) copy-start(f32[16]{0:T(128)} %far_gain_ref.1) | copy-start | bytes 196
  46.8 5.2 %collective-permute-start = (bf16[2,16,2304]{2,1,0:T(8,128)(2,1)S(1)}, bf16[2,16,2304]{2,1,0:T(8,128)(2,1)S(1)}, u32[]{:S(2)}, u32[]{:S(2)}) collective-permute-start(bf16[2,16,2304]{2,1,0:T(8,128)(2,1)S(1)} %get-tuple-element.8), channel_id=1, source_target_pairs={{0,1},{1,0},{2,3},{3,2},{4,5},{5,4},{6,7},{7,6},{8,9},{9,8},{10,11... | collective-permute-start | bytes 442376 | tf_op jit(solution)/shard_map/ppermute | solution.py:491

commit v4 on v3

--- a/solution.py
+++ b/solution.py
@@ -22,13 +22,14 @@
 N_Z = 16
 N_XY = 16
 COLS = WIN_BLOCKS + 2
-SPAN = HALF + 256
+SPAN = HALF + 128
 PAYLOAD = 640
 STRIP = 16
 BATCH = 4
 STORED = 3
+INLINE = BATCH - STORED
 TILES = HALF // 128
-GROUP = 4
+GROUP = 8
 STAGES = 4
 BIG = 60 * 1024 * 1024
 FILTER_VMEM = 46 * 1024 * 1024
@@ -37,7 +38,7 @@
 MSUN_SEC = 4.925491e-06
 SAMPLE_RATE = 2048.0
 
-Z_ORDER = [8, 10, 12, 14, 0, 2, 4, 6, 9, 11, 13, 15, 1, 3, 5, 7]
+Z_ORDER = [9, 11, 13, 15, 1, 3, 5, 7, 8, 10, 12, 14, 0, 2, 4, 6]
 XY_ORDER = [(k + 5) % N_XY for k in range(N_XY)]
 
 
@@ -49,8 +50,8 @@
 
 def constant_tables():
     rows = np.array([[q * N_Z + z for z in Z_ORDER] for q in XY_ORDER])
-    even, odd = rows[:, :8].reshape(-1), rows[:, 8:].reshape(-1)
-    k1 = np.concatenate([even, odd])
+    odd, even = rows[:, :8].reshape(-1), rows[:, 8:].reshape(-1)
+    k1 = np.concatenate([odd, even])
     k2 = np.arange(DFT_COLS)
     bins = 256 * k1[None, :] + k2[:, None]
     freq = np.maximum(bins * (SAMPLE_RATE / SAMPLES), 1.0)
@@ -71,7 +72,7 @@
         c, s = np.cos(angle), np.sin(angle)
         return np.concatenate([np.concatenate([c, s], 1), np.concatenate([-s, c], 1)], 0)
 
-    first_tables = np.stack([first(even), first(odd)])
+    first_tables = np.stack([first(odd), first(even)])
     angle = 2.0 * np.pi / SAMPLES * (k2[:, None] * t1[None, :] % SAMPLES)
     twist = np.stack([np.cos(angle), np.sin(angle)]).astype(np.float32)
     t2 = DFT_COLS // 2 - WIN_BLOCKS // 2 - 1 + np.arange(COLS)
@@ -117,7 +118,6 @@
 
 ROOT2 = math.sqrt(2.0)
 SIN_FIT = even_fit(lambda r: ROOT2 * np.pi * np.sinc(r), 5)
-COS_FIT = even_fit(lambda r: ROOT2 * np.cos(np.pi * r), 5)
 ROUND_SHIFT = 12582912.0
 
 
@@ -166,9 +166,11 @@
     rest = turns - ((turns + ROUND_SHIFT) - ROUND_SHIFT)
     square = rest * rest
     half_sin = horner(SIN_FIT, square) * rest
-    half_cos = horner(COS_FIT, square)
+    cosine = 1.0 - half_sin * half_sin
+    above = jnp.maximum(1.0 + cosine, 1e-12)
+    half_cos = above * lax.rsqrt(above)
     envelope = powers[3, here, :] * jnp.exp2(steep * powers[4, here, :])
-    return envelope * (1.0 - half_sin * half_sin), envelope * (half_sin * half_cos)
+    return envelope * cosine, envelope * (half_sin * half_cos)
 
 
 def wave_kernel(indices_ref, counts_ref, scalars_ref, powers_hbm, waves_ref, powers, staged, sems):
@@ -189,7 +191,7 @@
 
     @pl.loop(0, steps)
     def _(step):
-        slot = step // STORED * BATCH + step % STORED
+        slot = step // STORED * BATCH + INLINE + step % STORED
         coefs = slot_scalars(slot, indices_ref, scalars_ref)
 
         @pl.when(step >= STAGES)
@@ -278,15 +280,15 @@
     series[...] = jnp.zeros_like(series)
 
     def multiply(batch, place):
-        if place < STORED:
-            step = batch * STORED + place
+        if place >= INLINE:
+            step = batch * STORED + place - INLINE
             buffer = step % (2 * STORED)
             fetch(step).wait()
         else:
             coefs = slot_scalars(batch * BATCH + place, indices_ref, scalars_ref)
         for i in range(0, DFT_COLS, STRIP):
             here, there = slice(i, i + STRIP), slice(256 * place + i, 256 * place + i + STRIP)
-            if place < STORED:
+            if place >= INLINE:
                 cosine = waves[buffer, 0, here, :].astype(jnp.float32)
                 sine = waves[buffer, 1, here, :].astype(jnp.float32)
             else:
@@ -303,8 +305,8 @@
         for i in range(0, DFT_COLS, STRIP):
             here, below = slice(i, i + STRIP), slice(256 + i, 256 + i + STRIP)
             there = slice(256 * place + i, 256 * place + i + STRIP)
-            even_re, even_im = middle[0, there, 0:256], middle[0, there, 256:512]
-            odd_re, odd_im = middle[1, there, 0:256], middle[1, there, 256:512]
+            odd_re, odd_im = middle[0, there, 0:256], middle[0, there, 256:512]
+            even_re, even_im = middle[1, there, 0:256], middle[1, there, 256:512]
             c, s = twist_ref[0, here, :], twist_ref[1, here, :]
             for side in range(2):
                 lanes = slice(256 * side, 256 * side + 256)
@@ -350,18 +352,30 @@
         for place in range(BATCH):
             finish(batch * BATCH + place, place)
 
-    def write(out_ref, half):
+    def write(out_ref, half, shifted):
+        def tile_of(part, index):
+            column, tile = divmod(index, 4)
+            start = (part * COLS + 4 * half + column) * TPL_DEV
+            return series[tile, pl.ds(pl.multiple_of(start, TPL_DEV), TPL_DEV), :]
+
+        lower = lax.broadcasted_iota(jnp.int32, (TPL_DEV, 128), 1) < 64
         for part in range(2):
-            start = (part * COLS + 4 * half) * TPL_DEV
+            before = None
             for i in range(SPAN // 128):
-                column, tile = divmod(i + 3, 4)
-                rows = pl.ds(pl.multiple_of(start + column * TPL_DEV, TPL_DEV), TPL_DEV)
-                out_ref[part, :, 128 * i : 128 * i + 128] = series[tile, rows, :].astype(
-                    jnp.bfloat16
-                )
-
-    write(own_ref, half_ref[0])
-    write(send_ref, 1 - half_ref[0])
+                tile = tile_of(part, 4 + i)
+                if shifted:
+                    if before is None:
+                        before = pltpu.roll(tile_of(part, 3), 64, axis=1)
+                    turned = pltpu.roll(tile, 64, axis=1)
+                    tile, before = jnp.where(lower, before, turned), turned
+                out_ref[part, :, 128 * i : 128 * i + 128] = tile.astype(jnp.bfloat16)
+
+    for det in range(2):
+
+        @pl.when(half_ref[0] == det)
+        def _():
+            write(own_ref, det, det == 1)
+            write(send_ref, 1 - det, det == 1)
 
 
 def coherent_kernel(
@@ -373,59 +387,59 @@
     got_ref,
     out_ref,
     near,
-    far,
+    pairs,
     tiles,
     sems,
 ):
     def unpack(near_ref, far_ref):
-        for part in range(2):
-            near[part] = near_ref[part, :, 128 : 128 + HALF].astype(jnp.float32)
-            far[part] = far_ref[part].astype(jnp.float32)[:, 64 : 64 + HALF + 128]
+        for tile in range(TILES):
+            for part in range(2):
+                rows = slice(32 * tile + 16 * part, 32 * tile + 16 * part + 16)
+                near[rows, :] = near_ref[part, :, 128 * tile : 128 * tile + 128].astype(jnp.float32)
+                pairs[rows, :] = far_ref[part, :, 128 * tile : 128 * tile + 256]
 
     @pl.when(half_ref[0] == 0)
     def _():
-        unpack(own_ref, got_ref)
+        unpack(own_ref, got_ref.at[1])
 
     @pl.when(half_ref[0] == 1)
     def _():
-        unpack(got_ref, own_ref)
-
-    lane_id = lax.broadcasted_iota(jnp.int32, (8, 128), 1)
+        unpack(got_ref.at[0], own_ref)
+
+    row_id = lax.broadcasted_iota(jnp.int32, (256, 256), 0)
+    col_id = lax.broadcasted_iota(jnp.int32, (256, 256), 1)
 
     def copy_out(tile):
-        lanes = pl.ds(pl.multiple_of(tile * 128, 128), 128)
+        lanes = slice(128 * tile, 128 * tile + 128)
         return pltpu.make_async_copy(tiles.at[tile], out_ref.at[:, lanes], sems.at[tile])
 
-    @pl.loop(0, TILES // GROUP)
-    def _(group):
-        first_lane = pl.multiple_of(group * GROUP * 128, 128)
-        for sky in range(SKY):
-            shift = delay_ref[sky] + 64
-            gain_near, gain_far = near_gain_ref[sky], far_gain_ref[sky]
-            power = gain_near * gain_near + gain_far * gain_far
-            inverse = lax.rsqrt(jnp.full((1, 128), power, jnp.float32))
-            near_row = jnp.broadcast_to(gain_near * inverse, (8, 128))
-            far_row = jnp.broadcast_to(gain_far * inverse, (8, 128))
-            keep = lane_id < 128 - shift
-            for upper in (0, 8):
-                rows = slice(upper, upper + 8)
-                total = [None] * GROUP
-                for part in range(2):
-                    rolled = [
-                        pltpu.roll(far[part, rows, pl.ds(first_lane + 128 * i, 128)], 128 - shift, axis=1)
-                        for i in range(GROUP + 1)
-                    ]
-                    for i in range(GROUP):
-                        shifted = jnp.where(keep, rolled[i], rolled[i + 1])
-                        own = near[part, rows, pl.ds(first_lane + 128 * i, 128)]
-                        mixed = near_row * own + far_row * shifted
-                        squared = mixed * mixed
-                        total[i] = squared if part == 0 else total[i] + squared
+    for group in range(0, TILES, GROUP):
+        for sky in range(0, SKY, 2):
+            shift = jnp.where(col_id < 128, delay_ref[sky] + 64, delay_ref[sky + 1] - 64)
+            pick = jnp.where(row_id == col_id + shift, 1.0, 0.0).astype(jnp.bfloat16)
+            delayed = jnp.dot(
+                pairs[32 * group : 32 * (group + GROUP), :],
+                pick,
+                preferred_element_type=jnp.float32,
+            )
+            for side in range(2):
+                gain_near, gain_far = near_gain_ref[sky + side], far_gain_ref[sky + side]
+                power = gain_near * gain_near + gain_far * gain_far
+                inverse = lax.rsqrt(jnp.full((1, 128), power, jnp.float32))
+                near_row = jnp.broadcast_to(gain_near * inverse, (TPL_DEV, 128))
+                far_row = jnp.broadcast_to(gain_far * inverse, (TPL_DEV, 128))
+                lanes = slice(128 * side, 128 * side + 128)
                 for i in range(GROUP):
-                    place = pl.ds(sky + SKY * upper, 8, stride=SKY)
-                    tiles[group * GROUP + i, place, :] = total[i]
+                    tile = group + i
+                    re, im = (
+                        near_row * near[32 * tile + at : 32 * tile + at + 16, :]
+                        + far_row * delayed[32 * i + at : 32 * i + at + 16, lanes]
+                        for at in (0, 16)
+                    )
+                    place = pl.ds(sky + side, TPL_DEV, stride=SKY)
+                    tiles[tile, place, :] = re * re + im * im
         for i in range(GROUP):
-            copy_out(group * GROUP + i).start()
+            copy_out(group + i).start()
 
     for tile in range(TILES):
         copy_out(tile).wait()
@@ -488,15 +502,15 @@
         ],
         compiler_params=pltpu.CompilerParams(vmem_limit_bytes=FILTER_VMEM),
     )(indices, counts, half, scalars, plane, first_tables, twist, last, powers, waves)
-    got = lax.ppermute(send, "det", [(0, 1), (1, 0)])
+    got = lax.all_gather(send, "det", axis=0)
     out = pl.pallas_call(
         coherent_kernel,
         out_shape=jax.ShapeDtypeStruct((TPL_DEV * SKY, HALF), jnp.float32),
         in_specs=[SMEM] * 4 + [VMEM] * 2,
         out_specs=pl.BlockSpec(memory_space=pl.ANY),
         scratch_shapes=[
-            pltpu.VMEM((2, TPL_DEV, HALF), jnp.float32),
-            pltpu.VMEM((2, TPL_DEV, HALF + 128), jnp.float32),
+            pltpu.VMEM((2 * TPL_DEV * TILES, 128), jnp.float32),
+            pltpu.VMEM((2 * TPL_DEV * TILES, 256), jnp.bfloat16),
             pltpu.VMEM((TILES, TPL_DEV * SKY, 128), jnp.float32),
             pltpu.SemaphoreType.DMA((TILES,)),
         ],

time: 56 us -> 55.9 us (level)
  the two profiles are of different devices: /device:TPU:69 before, /device:TPU:7 now
where the time goes in v4:
time: 55.9 us; the launch traced here: 55.5 us
  blocking collectives  24.9 us (45%)
  Pallas kernels  22.7 us (41%)
  starting transfers between devices  7.01 us (13%)
  between operations  0.8 us (1%)
    all_to_all x1, blocking collectives, on_device(): line = lax.all_to_all(payload, 'bank', 0, 0, axis_index_groups=z_groups)  21 us
    pallas_call x1, Pallas kernels, on_device(): pl.pallas_call(filter_kernel, out_shape=(window, window), in_specs=[SMEM]...  9.55 us
    pallas_call x1, Pallas kernels, on_device(): pl.pallas_call(wave_kernel, out_shape=jax.ShapeDtypeStruct((WAVE_ROOM, 2,...  7.12 us
    all_to_all x1, starting transfers between devices, on_device(): plane = lax.all_to_all(spread, 'bank', 0, 0, axis_index_groups=xy_groups)  7.01 us
    all_gather x1, blocking collectives, on_device(): got = lax.all_gather(send, 'det', axis=0)  3.91 us
    pallas_call x1, Pallas kernels, on_device(): pl.pallas_call(coherent_kernel, out_shape=jax.ShapeDtypeStruct((TPL_DEV *...  2.98 us
    pallas_call x1, Pallas kernels, on_device(): pl.pallas_call(spread_kernel, out_shape=jax.ShapeDtypeStruct((N_XY, N_Z,...  1.55 us
    pallas_call x1, Pallas kernels, on_device(): pl.pallas_call(prepare_kernel, out_shape=jax.ShapeDtypeStruct((N_Z, 1, PA...  1.51 us
  transfers between devices with their start and end apart: 1, of which 0 were waited for; matrix products, arithmetic and copies ran while one was open for 0% of the time, Pallas kernels for 13%

profile of v4, /device:TPU:7, one launch (start us, length us, event | category | flops | bytes accessed | tf_op | source)
XLA Modules:
  0.0 55.5 jit_solution(15790616666781377126)
XLA Ops:
  0.0 1.5 %shard_map.118 = f32[16,1,640]{2,1,0:T(1,128)} custom-call(s32[1]{0:T(128)} %bitcast.1.bank_ref, f32[2,256]{1,0:T(2,128)} %bitcast.6, f32[1,256]{1,0:T(1,128)} %asd_ref.1), custom_call_target="tpu_custom_call" | custom-call | tf_op jit(solution)/shard_map/pallas_call | solution.py:458
  1.5 21.0 %all_to_all.10.line_ref = f32[16,1,640]{2,1,0:T(1,128)} all-to-all(f32[16,1,640]{2,1,0:T(1,128)} %shard_map.118), channel_id=1, replica_groups={{18,22,26,30,2,6,10,14,16,20,24,28,0,4,8,12},{50,54,58,62,34,38,42,46,4..., dimensions={0} | all-to-all | bytes 81920 | tf_op jit(solution)/shard_map/all_to_all | solution.py:465
  22.5 1.6 %shard_map.119 = bf16[16,16,640]{2,1,0:T(8,128)(2,1)} custom-call(f32[16,1,640]{2,1,0:T(1,128)} %all_to_all.10.line_ref), custom_call_target="tpu_custom_call" | custom-call | tf_op jit(solution)/shard_map/pallas_call | solution.py:466
  24.0 7.0 %all-to-all-start.1 = ((bf16[16,16,640]{2,1,0:T(8,128)(2,1)}), bf16[16,16,640]{2,1,0:T(8,128)(2,1)S(1)}, u32[]{:S(2)}, u32[]{:S(2)}) async-start(bf16[16,16,640]{2,1,0:T(8,128)(2,1)} %shard_map.119), calls=%async_computation.1 | async-start | bytes 655360 | tf_op jit(solution)/shard_map/all_to_all | solution.py:472
  31.7 0.0 copy-start
  31.7 0.0 copy-start.1
  31.7 0.0 copy-start.2
  31.7 0.0 copy-start.3
  31.7 0.0 copy-start.4
  31.8 0.0 copy-start.5
  31.8 7.1 %shard_map.120.waves_ref = bf16[80,2,256,256]{3,2,1,0:T(8,128)(2,1)} custom-call(s32[16]{0:T(128)} %indices_ref.3, s32[1]{0:T(128)S(6)} %copy.13.counts_ref, f32[8,64]{1,0:T(8,128)} %constant.18.clone.scalars_ref, f32[5,256,256]{2,1,0:T(8,128)} %constant.19.clone.powers_hbm.powers_ref), custom_call_target="tpu_custom_call" | custom-call | flops 41943040 | bytes 10485760 | tf_op jit(solution)/shard_map/pallas_call | solution.py:473
  38.9 0.0 all-to-all-done.1.gathered_ref
  38.9 0.0 copy-done
  38.9 0.0 copy-done.1
  38.9 0.0 copy-done.2
  38.9 0.0 copy-done.3
  38.9 0.0 copy-done.4
  38.9 0.0 copy-done.5
  39.0 0.0 copy-start.6
  39.0 0.0 copy-start.7
  39.0 0.0 copy-start.8
  39.0 9.6 %shard_map.121 = (bf16[2,16,2176]{2,1,0:T(8,128)(2,1)S(1)}, bf16[2,16,2176]{2,1,0:T(8,128)(2,1)S(1)}) custom-call(s32[16]{0:T(128)S(1)} %copy-done.5, s32[1]{0:T(128)S(6)} %copy.13.counts_ref, s32[1]{0:T(128)} %bitcast.half_ref, f32[8,64]{1,0:T(8,128)S(1)} %copy-done.4, bf16[16,16,640]{2,1,0:T(8,128)(2,1)S(1)} %all-to-all-done.1.gathered_ref, ...), custom_call_target="tpu_custom_call" | custom-call | tf_op jit(solution)/shard_map/pallas_call | solution.py:489
  48.6 3.9 %all-gather = bf16[4,16,2176]{2,1,0:T(8,128)(2,1)S(1)} all-gather(bf16[2,16,2176]{2,1,0:T(8,128)(2,1)S(1)} %get-tuple-element.8), channel_id=2, replica_groups=mesh['bank'=256,'det'=2] {'det'}, dimensions={0}, use_global_device_ids=true | all-gather | bytes 417792 | tf_op jit(solution)/shard_map/all_gather | solution.py:505
  52.5 0.0 copy-done.6
  52.5 0.0 copy-done.7
  52.5 0.0 copy-done.8
  52.5 3.0 %shard_map.122 = f32[256,2048]{1,0:T(8,128)} custom-call(s32[1]{0:T(128)} %bitcast.half_ref, s32[16]{0:T(128)S(1)} %copy-done.6, f32[16]{0:T(128)S(1)} %copy-done.7, f32[16]{0:T(128)S(1)} %copy-done.8, bf16[2,16,2176]{2,1,0:T(8,128)(2,1)S(1)} %get-tuple-element.7.own_ref, bf16[2,2,16,2176]{3,2,1,0:T(8,128)(2,1)S(1)} %bitcast.5), custom_call_target="tpu_custom_call" | custom-call | tf_op jit(solution)/shard_map/pallas_call | solution.py:506
Async XLA Ops:
  24.0 14.9 %all-to-all-start.1 = ((bf16[16,16,640]{2,1,0:T(8,128)(2,1)}), bf16[16,16,640]{2,1,0:T(8,128)(2,1)S(1)}, u32[]{:S(2)}, u32[]{:S(2)}) async-start(bf16[16,16,640]{2,1,0:T(8,128)(2,1)} %shard_map.119), calls=%async_computation.1 | async-start | bytes 655360 | tf_op jit(solution)/shard_map/all_to_all | solution.py:472
  31.7 7.2 %copy-start = (f32[5,256,256]{2,1,0:T(8,128)S(1)}, f32[5,256,256]{2,1,0:T(8,128)}, u32[]{:S(2)}) copy-start(f32[5,256,256]{2,1,0:T(8,128)} %constant.19.clone.powers_hbm.powers_ref) | copy-start | bytes 3932164
  31.7 7.2 %copy-start.1 = (f32[2,256,256]{2,1,0:T(8,128)S(1)}, f32[2,256,256]{2,1,0:T(8,128)}, u32[]{:S(2)}) copy-start(f32[2,256,256]{2,1,0:T(8,128)} %constant.21.clone.twist_ref) | copy-start | bytes 1572868
  31.7 7.2 %copy-start.2 = (bf16[2,256,512]{2,1,0:T(8,128)(2,1)S(1)}, bf16[2,256,512]{2,1,0:T(8,128)(2,1)}, u32[]{:S(2)}) copy-start(bf16[2,256,512]{2,1,0:T(8,128)(2,1)} %constant.20.clone.first_ref) | copy-start | bytes 1572868
  31.7 7.2 %copy-start.3 = (bf16[2,32,512]{2,1,0:T(8,128)(2,1)S(1)}, bf16[2,32,512]{2,1,0:T(8,128)(2,1)}, u32[]{:S(2)}) copy-start(bf16[2,32,512]{2,1,0:T(8,128)(2,1)} %constant.22.clone.last_ref) | copy-start | bytes 196612
  31.7 7.2 %copy-start.4 = (f32[8,64]{1,0:T(8,128)S(1)}, f32[8,64]{1,0:T(8,128)}, u32[]{:S(2)}) copy-start(f32[8,64]{1,0:T(8,128)} %constant.18.clone.scalars_ref) | copy-start | bytes 6148
  31.8 7.2 %copy-start.5 = (s32[16]{0:T(128)S(1)}, s32[16]{0:T(128)}, u32[]{:S(2)}) copy-start(s32[16]{0:T(128)} %indices_ref.3) | copy-start | bytes 196
  39.0 13.5 %copy-start.6 = (s32[16]{0:T(128)S(1)}, s32[16]{0:T(128)}, u32[]{:S(2)}) copy-start(s32[16]{0:T(128)} %delay_ref.1) | copy-start | bytes 196
  39.0 13.5 %copy-start.7 = (f32[16]{0:T(128)S(1)}, f32[16]{0:T(128)}, u32[]{:S(2)}) copy-start(f32[16]{0:T(128)} %near_gain_ref.1) | copy-start | bytes 196
  39.0 13.5 %copy-start.8 = (f32[16]{0:T(128)S(1)}, f32[16]{0:T(128)}, u32[]{:S(2)}) copy-start(f32[16]{0:T(128)} %far_gain_ref.1) | copy-start | bytes 196

commit v5 on v4

--- a/solution.py
+++ b/solution.py
@@ -26,8 +26,7 @@
 PAYLOAD = 640
 STRIP = 16
 BATCH = 4
-STORED = 3
-INLINE = BATCH - STORED
+EARLY = 5
 TILES = HALF // 128
 GROUP = 8
 STAGES = 4
@@ -130,7 +129,7 @@
 
 def payload_row(bank, strain, asd):
     weight = asd * asd
-    over = (strain * weight).astype(jnp.bfloat16).astype(jnp.float32)
+    over = strain * weight
     bin_id = bank * 256 + lax.broadcasted_iota(jnp.int32, (1, 256), 1)
     clipped = jnp.maximum(bin_id.astype(jnp.float32) * (SAMPLE_RATE / SAMPLES), 1.0)
     square = clipped * clipped
@@ -173,12 +172,32 @@
     return envelope * cosine, envelope * (half_sin * half_cos)
 
 
-def wave_kernel(indices_ref, counts_ref, scalars_ref, powers_hbm, waves_ref, powers, staged, sems):
-    steps = rounded_up(counts_ref[0]) // BATCH * STORED
-
-    def store(step):
-        place = step % STAGES
-        return pltpu.make_async_copy(staged.at[place], waves_ref.at[step], sems.at[place])
+def early_slots(bank, count):
+    z = bank % N_Z
+    early = jnp.where(z < 4, EARLY, jnp.where(z < 7, EARLY // 2, 0))
+    return jnp.minimum(early, rounded_up(count))
+
+
+def wave_kernel(
+    bank_ref,
+    indices_ref,
+    counts_ref,
+    scalars_ref,
+    powers_hbm,
+    early_ref,
+    waves_ref,
+    powers,
+    staged,
+    sems,
+):
+    first, last = early_slots(bank_ref[0], counts_ref[0]), rounded_up(counts_ref[0])
+    write_waves(first, last, indices_ref, scalars_ref, powers_hbm, waves_ref, powers, staged, sems)
+
+
+def write_waves(first, last, indices_ref, scalars_ref, powers_hbm, waves_ref, powers, staged, sems):
+    def store(slot):
+        place = slot % STAGES
+        return pltpu.make_async_copy(staged.at[place], waves_ref.at[slot], sems.at[place])
 
     def load(strip):
         rows = pl.ds(strip * 64, 64)
@@ -186,64 +205,73 @@
             powers_hbm.at[:, rows], powers.at[:, rows], sems.at[STAGES + strip]
         )
 
-    for strip in range(4):
-        load(strip).start()
-
-    @pl.loop(0, steps)
-    def _(step):
-        slot = step // STORED * BATCH + INLINE + step % STORED
+    @pl.when(last > first)
+    def _():
+        for strip in range(4):
+            load(strip).start()
+
+    @pl.loop(first, last)
+    def _(slot):
         coefs = slot_scalars(slot, indices_ref, scalars_ref)
 
-        @pl.when(step >= STAGES)
+        @pl.when(slot >= first + STAGES)
         def _():
-            store(step - STAGES).wait()
+            store(slot - STAGES).wait()
 
         @pl.loop(0, DFT_COLS // 64)
         def _(strip):
-            @pl.when(step == 0)
+            @pl.when(slot == first)
             def _():
                 load(strip).wait()
 
             for piece in range(4):
                 here = pl.ds(pl.multiple_of(strip * 64 + piece * 16, 16), 16)
                 cosine, sine = wave(coefs, powers, here)
-                staged[step % STAGES, 0, here, :] = cosine.astype(jnp.bfloat16)
-                staged[step % STAGES, 1, here, :] = sine.astype(jnp.bfloat16)
-
-        store(step).start()
+                staged[slot % STAGES, 0, here, :] = cosine.astype(jnp.bfloat16)
+                staged[slot % STAGES, 1, here, :] = sine.astype(jnp.bfloat16)
+
+        store(slot).start()
 
     for back in range(STAGES, 0, -1):
 
-        @pl.when(steps >= back)
+        @pl.when(last - first >= back)
         def _():
-            store(steps - back).wait()
+            store(last - back).wait()
 
 
 def rounded_up(count):
     return (count + BATCH - 1) // BATCH * BATCH
 
 
-def prepare_kernel(bank_ref, strain_ref, asd_ref, out_ref):
+def prepare_kernel(
+    bank_ref,
+    indices_ref,
+    counts_ref,
+    scalars_ref,
+    strain_ref,
+    asd_ref,
+    powers_hbm,
+    out_ref,
+    waves_ref,
+    powers,
+    staged,
+    sems,
+):
     row = payload_row(bank_ref[0], strain_ref[...], asd_ref[...])
-    out_ref[...] = jnp.broadcast_to(row[:, None, :], (N_Z, 1, PAYLOAD))
-
-
-def spread_kernel(line_ref, out_ref):
-    line = line_ref[...].reshape(N_Z, PAYLOAD).astype(jnp.bfloat16)
-    for i in range(N_XY):
-        out_ref[i] = line
+    pair = jnp.concatenate([row[:, : PAYLOAD // 2], row[:, PAYLOAD // 2 :]], axis=0)
+    out_ref[...] = jnp.broadcast_to(pair.astype(jnp.bfloat16)[None], out_ref.shape)
+    last = early_slots(bank_ref[0], counts_ref[0])
+    write_waves(0, last, indices_ref, scalars_ref, powers_hbm, waves_ref, powers, staged, sems)
 
 
 def filter_kernel(
     indices_ref,
     counts_ref,
     half_ref,
-    scalars_ref,
     gathered_ref,
     first_ref,
     twist_ref,
     last_ref,
-    powers_ref,
     waves_ref,
     own_ref,
     send_ref,
@@ -256,16 +284,17 @@
     sems,
 ):
     count = counts_ref[0]
-    batches = rounded_up(count) // BATCH
-    steps = batches * STORED
-
-    def fetch(step):
-        place = step % (2 * STORED)
-        return pltpu.make_async_copy(waves_ref.at[step], waves.at[place], sems.at[place])
-
-    @pl.loop(0, jnp.minimum(steps, 2 * STORED))
-    def _(step):
-        fetch(step).start()
+    slots = rounded_up(count)
+
+    def fetch(slot):
+        place = slot % (2 * BATCH)
+        return pltpu.make_async_copy(waves_ref.at[slot], waves.at[place], sems.at[place])
+
+    def fetch_batch(batch):
+        for place in range(BATCH):
+            fetch(batch * BATCH + place).start()
+
+    fetch_batch(0)
 
     for part in range(2):
         block = gathered_ref[:, :, 256 * part : 256 * part + 256].astype(jnp.float32)
@@ -279,20 +308,13 @@
     lane_id = lax.broadcasted_iota(jnp.int32, (1, MASSES), 1)
     series[...] = jnp.zeros_like(series)
 
-    def multiply(batch, place):
-        if place >= INLINE:
-            step = batch * STORED + place - INLINE
-            buffer = step % (2 * STORED)
-            fetch(step).wait()
-        else:
-            coefs = slot_scalars(batch * BATCH + place, indices_ref, scalars_ref)
+    def multiply(slot, place):
+        buffer = slot % (2 * BATCH)
+        fetch(slot).wait()
         for i in range(0, DFT_COLS, STRIP):
             here, there = slice(i, i + STRIP), slice(256 * place + i, 256 * place + i + STRIP)
-            if place >= INLINE:
-                cosine = waves[buffer, 0, here, :].astype(jnp.float32)
-                sine = waves[buffer, 1, here, :].astype(jnp.float32)
-            else:
-                cosine, sine = wave(coefs, powers_ref, here)
+            cosine = waves[buffer, 0, here, :].astype(jnp.float32)
+            sine = waves[buffer, 1, here, :].astype(jnp.float32)
             re, im = spectrum[0, here, :], spectrum[1, here, :]
             real_part = (re * cosine - im * sine).astype(jnp.bfloat16)
             imag_part = (re * sine + im * cosine).astype(jnp.bfloat16)
@@ -331,18 +353,14 @@
                     :, 128 * i : 128 * i + 128
                 ]
 
-    @pl.loop(0, batches)
+    @pl.loop(0, slots // BATCH)
     def _(batch):
+        @pl.when((batch + 1) * BATCH < slots)
+        def _():
+            fetch_batch(batch + 1)
+
         for place in range(BATCH):
-            multiply(batch, place)
-
-        for place in range(STORED):
-            later = (batch + 2) * STORED + place
-
-            @pl.when(later < steps)
-            def _():
-                fetch(later).start()
-
+            multiply(batch * BATCH + place, place)
         for parity in range(2):
             middle[parity] = jnp.dot(
                 products[parity], first_ref[parity], preferred_element_type=jnp.float32
@@ -455,41 +473,40 @@
     z_groups, xy_groups = group_lists()
     bank = lax.axis_index("bank").astype(jnp.int32)[None]
     half = lax.axis_index("det").astype(jnp.int32)[None]
-    payload = pl.pallas_call(
+    room = jax.ShapeDtypeStruct((WAVE_ROOM, 2, DFT_COLS, 256), jnp.bfloat16)
+    wave_scratch = [
+        pltpu.VMEM((5, DFT_COLS, 256), jnp.float32),
+        pltpu.VMEM((STAGES, 2, DFT_COLS, 256), jnp.bfloat16),
+        pltpu.SemaphoreType.DMA((STAGES + 4,)),
+    ]
+    payload, early = pl.pallas_call(
         prepare_kernel,
-        out_shape=jax.ShapeDtypeStruct((N_Z, 1, PAYLOAD), jnp.float32),
-        in_specs=[SMEM, VMEM, VMEM],
-        out_specs=VMEM,
+        out_shape=(jax.ShapeDtypeStruct((N_Z, 2, PAYLOAD // 2), jnp.bfloat16), room),
+        in_specs=[SMEM] * 4 + [VMEM] * 2 + [ANY],
+        out_specs=(VMEM, ANY),
+        scratch_shapes=wave_scratch,
         compiler_params=pltpu.CompilerParams(vmem_limit_bytes=BIG),
-    )(bank, strain[0], asd_inv)
+    )(bank, indices, counts, scalars, strain[0], asd_inv, powers)
     line = lax.all_to_all(payload, "bank", 0, 0, axis_index_groups=z_groups)
-    spread = pl.pallas_call(
-        spread_kernel,
-        out_shape=jax.ShapeDtypeStruct((N_XY, N_Z, PAYLOAD), jnp.bfloat16),
-        in_specs=[VMEM],
-        out_specs=VMEM,
-    )(line)
+    spread = jnp.broadcast_to(line.reshape(1, N_Z, PAYLOAD), (N_XY, N_Z, PAYLOAD))
     plane = lax.all_to_all(spread, "bank", 0, 0, axis_index_groups=xy_groups)
     waves = pl.pallas_call(
         wave_kernel,
-        out_shape=jax.ShapeDtypeStruct((WAVE_ROOM, 2, DFT_COLS, 256), jnp.bfloat16),
-        in_specs=[SMEM] * 3 + [ANY],
+        out_shape=room,
+        in_specs=[SMEM] * 4 + [ANY] * 2,
         out_specs=ANY,
-        scratch_shapes=[
-            pltpu.VMEM((5, DFT_COLS, 256), jnp.float32),
-            pltpu.VMEM((STAGES, 2, DFT_COLS, 256), jnp.bfloat16),
-            pltpu.SemaphoreType.DMA((STAGES + 4,)),
-        ],
+        scratch_shapes=wave_scratch,
+        input_output_aliases={5: 0},
         cost_estimate=pl.CostEstimate(
             flops=40 * 2**20, bytes_accessed=10 * 2**20, transcendentals=2**20
         ),
         compiler_params=pltpu.CompilerParams(vmem_limit_bytes=BIG),
-    )(indices, counts, scalars, powers)
+    )(bank, indices, counts, scalars, powers, early)
     window = jax.ShapeDtypeStruct((2, TPL_DEV, SPAN), jnp.bfloat16)
     own, send = pl.pallas_call(
         filter_kernel,
         out_shape=(window, window),
-        in_specs=[SMEM] * 4 + [VMEM] * 5 + [ANY],
+        in_specs=[SMEM] * 3 + [VMEM] * 4 + [ANY],
         out_specs=(VMEM, VMEM),
         scratch_shapes=[
             pltpu.VMEM((2, DFT_COLS, 256), jnp.float32),
@@ -497,11 +514,11 @@
             pltpu.VMEM((2, BATCH * DFT_COLS, 512), jnp.float32),
             pltpu.VMEM((BATCH, 512, 512), jnp.bfloat16),
             pltpu.VMEM((4, 2 * COLS * TPL_DEV, 128), jnp.float32),
-            pltpu.VMEM((2 * STORED, 2, DFT_COLS, 256), jnp.bfloat16),
-            pltpu.SemaphoreType.DMA((2 * STORED,)),
+            pltpu.VMEM((2 * BATCH, 2, DFT_COLS, 256), jnp.bfloat16),
+            pltpu.SemaphoreType.DMA((2 * BATCH,)),
         ],
         compiler_params=pltpu.CompilerParams(vmem_limit_bytes=FILTER_VMEM),
-    )(indices, counts, half, scalars, plane, first_tables, twist, last, powers, waves)
+    )(indices, counts, half, plane, first_tables, twist, last, waves)
     got = lax.all_gather(send, "det", axis=0)
     out = pl.pallas_call(
         coherent_kernel,

time: 55.9 us -> 52 us (0.930)
  the two profiles are of different devices: /device:TPU:7 before, /device:TPU:57 now
where the time goes in v5:
time: 52 us; the launch traced here: 51.7 us
  Pallas kernels  23.5 us (45%)
  blocking collectives  19.8 us (38%)
  starting transfers between devices  6.75 us (13%)
  local copies, waits for them, and re-layouts  0.89 us (2%)
  between operations  0.77 us (1%)
    all_to_all x1, blocking collectives, on_device(): line = lax.all_to_all(payload, 'bank', 0, 0, axis_index_groups=z_groups)  15.9 us
    pallas_call x1, Pallas kernels, on_device(): pl.pallas_call(filter_kernel, out_shape=(window, window), in_specs=[SMEM]...  8.86 us
    all_to_all x1, starting transfers between devices, on_device(): plane = lax.all_to_all(spread, 'bank', 0, 0, axis_index_groups=xy_groups)  6.75 us
    pallas_call x1, Pallas kernels, on_device(): pl.pallas_call(wave_kernel, out_shape=room, in_specs=[SMEM] * 4 + [ANY] *...  6.68 us
    pallas_call x1, Pallas kernels, on_device(): pl.pallas_call(prepare_kernel, out_shape=(jax.ShapeDtypeStruct((N_Z, 2, P...  4.96 us
    all_gather x1, blocking collectives, on_device(): got = lax.all_gather(send, 'det', axis=0)  3.88 us
    pallas_call x1, Pallas kernels, on_device(): pl.pallas_call(coherent_kernel, out_shape=jax.ShapeDtypeStruct((TPL_DEV *...  3 us
  transfers between devices with their start and end apart: 1, of which 0 were waited for; matrix products, arithmetic and copies ran while one was open for 0% of the time, Pallas kernels for 13%

profile of v5, /device:TPU:57, one launch (start us, length us, event | category | flops | bytes accessed | tf_op | source)
XLA Modules:
  0.0 51.7 jit_solution(16906620397539151363)
XLA Ops:
  0.7 5.0 %shard_map.118 = (bf16[16,2,320]{2,1,0:T(2,128)(2,1)}, bf16[80,2,256,256]{3,2,1,0:T(8,128)(2,1)}) custom-call(s32[1]{0:T(128)} %bitcast.1.bank_ref, s32[16]{0:T(128)} %indices_ref.5, s32[1]{0:T(128)S(6)} %copy.15.counts_ref, f32[8,64]{1,0:T(8,128)} %constant.18.clone.scalars_ref, f32[2,256]{1,0:T(2,128)} %bitcast.6, f32[1,256]{1,0:T(1,128)} %asd_ref.1, ...), custom_call_target="tpu_custom_call" | custom-call | tf_op jit(solution)/shard_map/pallas_call | solution.py:482
  5.6 15.9 %all_to_all.10 = bf16[16,2,320]{2,1,0:T(2,128)(2,1)S(1)} all-to-all(bf16[16,2,320]{2,1,0:T(2,128)(2,1)} %get-tuple-element.9), channel_id=1, replica_groups={{18,22,26,30,2,6,10,14,16,20,24,28,0,4,8,12},{50,54,58,62,34,38,42,46,4..., dimensions={0} | all-to-all | bytes 40960 | tf_op jit(solution)/shard_map/all_to_all | solution.py:490
  21.5 0.1 broadcast_in_dim.15
  21.6 0.8 %broadcast_in_dim.16 = bf16[16,16,640]{2,1,0:T(8,128)(2,1)} broadcast(bf16[16,640]{1,0:T(8,128)(2,1)S(1)} %broadcast_in_dim.15), dimensions={1,2} | broadcast | bytes 348160 | tf_op jit(solution)/shard_map/broadcast_in_dim | solution.py:491
  22.4 6.8 %all-to-all-start.1 = ((bf16[16,16,640]{2,1,0:T(8,128)(2,1)}), bf16[16,16,640]{2,1,0:T(8,128)(2,1)S(1)}, u32[]{:S(2)}, u32[]{:S(2)}) async-start(bf16[16,16,640]{2,1,0:T(8,128)(2,1)} %broadcast_in_dim.16), calls=%async_computation.1 | async-start | bytes 655360 | tf_op jit(solution)/shard_map/all_to_all | solution.py:492
  29.1 0.0 copy-start
  29.1 0.0 copy-start.1
  29.1 0.0 copy-start.2
  29.1 0.0 copy-start.3
  29.2 6.7 %shard_map.119.waves_ref = bf16[80,2,256,256]{3,2,1,0:T(8,128)(2,1)} custom-call(s32[1]{0:T(128)} %bitcast.1.bank_ref, s32[16]{0:T(128)} %indices_ref.5, s32[1]{0:T(128)S(6)} %copy.15.counts_ref, f32[8,64]{1,0:T(8,128)} %constant.18.clone.scalars_ref, f32[5,256,256]{2,1,0:T(8,128)} %constant.19.clone.powers_hbm, ...), custom_call_target="tpu_custom_call", output_to_operand_aliasing={{}: (5, {})} | custom-call | flops 41943040 | bytes 10485760 | tf_op jit(solution)/shard_map/pallas_call | solution.py:493
  35.8 0.0 copy-start.4
  35.9 0.0 copy-start.5
  35.9 0.0 copy-start.6
  35.9 0.0 all-to-all-done.1.gathered_ref
  35.9 0.0 copy-done
  35.9 0.0 copy-done.1
  35.9 0.0 copy-done.2
  35.9 0.0 copy-done.3
  35.9 8.9 %shard_map.120 = (bf16[2,16,2176]{2,1,0:T(8,128)(2,1)S(1)}, bf16[2,16,2176]{2,1,0:T(8,128)(2,1)S(1)}) custom-call(s32[16]{0:T(128)S(1)} %copy-done.3, s32[1]{0:T(128)S(6)} %copy.15.counts_ref, s32[1]{0:T(128)} %bitcast.half_ref, bf16[16,16,640]{2,1,0:T(8,128)(2,1)S(1)} %all-to-all-done.1.gathered_ref, bf16[2,256,512]{2,1,0:T(8,128)(2,1)S(1)} %copy-done, ...), custom_call_target="tpu_custom_call" | custom-call | tf_op jit(solution)/shard_map/pallas_call | solution.py:506
  44.8 3.9 %all-gather = bf16[4,16,2176]{2,1,0:T(8,128)(2,1)S(1)} all-gather(bf16[2,16,2176]{2,1,0:T(8,128)(2,1)S(1)} %get-tuple-element.12), channel_id=2, replica_groups=mesh['bank'=256,'det'=2] {'det'}, dimensions={0}, use_global_device_ids=true | all-gather | bytes 417792 | tf_op jit(solution)/shard_map/all_gather | solution.py:522
  48.7 0.0 copy-done.4
  48.7 0.0 copy-done.5
  48.7 0.0 copy-done.6
  48.7 3.0 %shard_map.121 = f32[256,2048]{1,0:T(8,128)} custom-call(s32[1]{0:T(128)} %bitcast.half_ref, s32[16]{0:T(128)S(1)} %copy-done.4, f32[16]{0:T(128)S(1)} %copy-done.5, f32[16]{0:T(128)S(1)} %copy-done.6, bf16[2,16,2176]{2,1,0:T(8,128)(2,1)S(1)} %get-tuple-element.11.own_ref, bf16[2,2,16,2176]{3,2,1,0:T(8,128)(2,1)S(1)} %bitcast.5), custom_call_target="tpu_custom_call" | custom-call | tf_op jit(solution)/shard_map/pallas_call | solution.py:523
Async XLA Ops:
  22.4 13.5 %all-to-all-start.1 = ((bf16[16,16,640]{2,1,0:T(8,128)(2,1)}), bf16[16,16,640]{2,1,0:T(8,128)(2,1)S(1)}, u32[]{:S(2)}, u32[]{:S(2)}) async-start(bf16[16,16,640]{2,1,0:T(8,128)(2,1)} %broadcast_in_dim.16), calls=%async_computation.1 | async-start | bytes 655360 | tf_op jit(solution)/shard_map/all_to_all | solution.py:492
  29.1 6.8 %copy-start = (bf16[2,256,512]{2,1,0:T(8,128)(2,1)S(1)}, bf16[2,256,512]{2,1,0:T(8,128)(2,1)}, u32[]{:S(2)}) copy-start(bf16[2,256,512]{2,1,0:T(8,128)(2,1)} %constant.20.clone.first_ref) | copy-start | bytes 1572868
  29.1 6.8 %copy-start.1 = (f32[2,256,256]{2,1,0:T(8,128)S(1)}, f32[2,256,256]{2,1,0:T(8,128)}, u32[]{:S(2)}) copy-start(f32[2,256,256]{2,1,0:T(8,128)} %constant.21.clone.twist_ref) | copy-start | bytes 1572868
  29.1 6.8 %copy-start.2 = (bf16[2,32,512]{2,1,0:T(8,128)(2,1)S(1)}, bf16[2,32,512]{2,1,0:T(8,128)(2,1)}, u32[]{:S(2)}) copy-start(bf16[2,32,512]{2,1,0:T(8,128)(2,1)} %constant.22.clone.last_ref) | copy-start | bytes 196612
  29.1 6.8 %copy-start.3 = (s32[16]{0:T(128)S(1)}, s32[16]{0:T(128)}, u32[]{:S(2)}) copy-start(s32[16]{0:T(128)} %indices_ref.5) | copy-start | bytes 196
  35.8 12.8 %copy-start.4 = (s32[16]{0:T(128)S(1)}, s32[16]{0:T(128)}, u32[]{:S(2)}) copy-start(s32[16]{0:T(128)} %delay_ref.1) | copy-start | bytes 196
  35.9 12.8 %copy-start.5 = (f32[16]{0:T(128)S(1)}, f32[16]{0:T(128)}, u32[]{:S(2)}) copy-start(f32[16]{0:T(128)} %near_gain_ref.1) | copy-start | bytes 196
  35.9 12.8 %copy-start.6 = (f32[16]{0:T(128)S(1)}, f32[16]{0:T(128)}, u32[]{:S(2)}) copy-start(f32[16]{0:T(128)} %far_gain_ref.1) | copy-start | bytes 196

commit v6 on v5

--- a/solution.py
+++ b/solution.py
@@ -25,7 +25,8 @@
 SPAN = HALF + 128
 PAYLOAD = 640
 STRIP = 16
-BATCH = 4
+BATCH = 8
+LAST_ROWS = 24
 EARLY = 5
 TILES = HALF // 128
 GROUP = 8
@@ -75,13 +76,14 @@
     angle = 2.0 * np.pi / SAMPLES * (k2[:, None] * t1[None, :] % SAMPLES)
     twist = np.stack([np.cos(angle), np.sin(angle)]).astype(np.float32)
     t2 = DFT_COLS // 2 - WIN_BLOCKS // 2 - 1 + np.arange(COLS)
-    last = np.zeros((2, 32, 512))
+    last = np.zeros((2 * LAST_ROWS, 1024))
     for side in range(2):
         steps = k2[None, :] * (t2[:, None] * DFT_ROWS + 256 * side)
         angle = 2.0 * np.pi / SAMPLES * (steps % SAMPLES)
         c, s = np.cos(angle), np.sin(angle)
-        last[side, :COLS] = np.concatenate([c, -s], 1)
-        last[side, COLS : 2 * COLS] = np.concatenate([s, c], 1)
+        rows = np.concatenate([np.concatenate([c, -s], 1), np.concatenate([s, c], 1)], 0)
+        at = LAST_ROWS * side
+        last[at : at + 2 * COLS] = np.concatenate([-rows if side else rows, rows], 1)
 
     seconds = 6.0 * 1.03 ** np.arange(MASSES) * MSUN_SEC
     ratio = 0.16 + 0.09 * np.arange(64) / 63.0
@@ -323,34 +325,30 @@
                 products[parity, there, 0:128] = real_part[:, lanes]
                 products[parity, there, 128:256] = imag_part[:, lanes]
 
-    def twist(place):
+    def twist(place, parity):
         for i in range(0, DFT_COLS, STRIP):
-            here, below = slice(i, i + STRIP), slice(256 + i, 256 + i + STRIP)
+            here = slice(i, i + STRIP)
             there = slice(256 * place + i, 256 * place + i + STRIP)
-            odd_re, odd_im = middle[0, there, 0:256], middle[0, there, 256:512]
-            even_re, even_im = middle[1, there, 0:256], middle[1, there, 256:512]
+            upper, lower = middle[parity, there, 0:256], middle[parity, there, 256:512]
             c, s = twist_ref[0, here, :], twist_ref[1, here, :]
-            for side in range(2):
-                lanes = slice(256 * side, 256 * side + 256)
-                upper = even_re - odd_re if side else even_re + odd_re
-                lower = even_im - odd_im if side else even_im + odd_im
-                twisted[place, here, lanes] = (upper * c - lower * s).astype(jnp.bfloat16)
-                twisted[place, below, lanes] = (upper * s + lower * c).astype(jnp.bfloat16)
+            at = 512 * parity + i
+            twisted[place, at : at + STRIP] = (upper * c - lower * s).astype(jnp.bfloat16)
+            twisted[place, at + 256 : at + 256 + STRIP] = (upper * s + lower * c).astype(
+                jnp.bfloat16
+            )
 
     def finish(slot, place):
         mass = indices_ref[slot] % 64
         norm = jnp.sum(jnp.where(lane_id == mass, norm_row, 0.0), axis=1, keepdims=True)
         scale = lax.rsqrt(norm) * jnp.where(slot < count, 1.0, 0.0)
+        result = scale * jnp.dot(
+            last_ref[...], twisted[place], preferred_element_type=jnp.float32
+        )
         for side in range(2):
-            result = jnp.dot(
-                last_ref[side],
-                twisted[place, :, 256 * side : 256 * side + 256],
-                preferred_element_type=jnp.float32,
-            )
-            scaled = result[: 2 * COLS] * scale
+            rows = slice(LAST_ROWS * side, LAST_ROWS * side + 2 * COLS)
             for i in range(2):
-                series[2 * side + i, pl.ds(slot, 2 * COLS, stride=TPL_DEV), :] = scaled[
-                    :, 128 * i : 128 * i + 128
+                series[2 * side + i, pl.ds(slot, 2 * COLS, stride=TPL_DEV), :] = result[
+                    rows, 128 * i : 128 * i + 128
                 ]
 
     @pl.loop(0, slots // BATCH)
@@ -365,8 +363,9 @@
             middle[parity] = jnp.dot(
                 products[parity], first_ref[parity], preferred_element_type=jnp.float32
             )
-        for place in range(BATCH):
-            twist(place)
+        for parity in range(2):
+            for place in range(BATCH):
+                twist(place, parity)
         for place in range(BATCH):
             finish(batch * BATCH + place, place)
 
@@ -512,7 +511,7 @@
             pltpu.VMEM((2, DFT_COLS, 256), jnp.float32),
             pltpu.VMEM((2, BATCH * DFT_COLS, 256), jnp.bfloat16),
             pltpu.VMEM((2, BATCH * DFT_COLS, 512), jnp.float32),
-            pltpu.VMEM((BATCH, 512, 512), jnp.bfloat16),
+            pltpu.VMEM((BATCH, 1024, 256), jnp.bfloat16),
             pltpu.VMEM((4, 2 * COLS * TPL_DEV, 128), jnp.float32),
             pltpu.VMEM((2 * BATCH, 2, DFT_COLS, 256), jnp.bfloat16),
             pltpu.SemaphoreType.DMA((2 * BATCH,)),

time: 52 us -> 52 us (level)
  the two profiles are of different devices: /device:TPU:57 before, /device:TPU:31 now
where the time goes in v6:
time: 52 us; the launch traced here: 51.6 us
  Pallas kernels  22.1 us (42%)
  blocking collectives  21.2 us (41%)
  starting transfers between devices  6.67 us (13%)
  local copies, waits for them, and re-layouts  0.89 us (2%)
  between operations  0.77 us (1%)
    all_to_all x1, blocking collectives, on_device(): line = lax.all_to_all(payload, 'bank', 0, 0, axis_index_groups=z_groups)  17.3 us
    pallas_call x1, Pallas kernels, on_device(): pl.pallas_call(filter_kernel, out_shape=(window, window), in_specs=[SMEM]...  7.52 us
    pallas_call x1, Pallas kernels, on_device(): pl.pallas_call(wave_kernel, out_shape=room, in_specs=[SMEM] * 4 + [ANY] *...  6.68 us
    all_to_all x1, starting transfers between devices, on_device(): plane = lax.all_to_all(spread, 'bank', 0, 0, axis_index_groups=xy_groups)  6.67 us
    pallas_call x1, Pallas kernels, on_device(): pl.pallas_call(prepare_kernel, out_shape=(jax.ShapeDtypeStruct((N_Z, 2, P...  4.96 us
    all_gather x1, blocking collectives, on_device(): got = lax.all_gather(send, 'det', axis=0)  3.91 us
    pallas_call x1, Pallas kernels, on_device(): pl.pallas_call(coherent_kernel, out_shape=jax.ShapeDtypeStruct((TPL_DEV *...  2.98 us
  transfers between devices with their start and end apart: 1, of which 0 were waited for; matrix products, arithmetic and copies ran while one was open for 0% of the time, Pallas kernels for 13%

profile of v6, /device:TPU:31, one launch (start us, length us, event | category | flops | bytes accessed | tf_op | source)
XLA Modules:
  0.0 51.6 jit_solution(15232473220781016836)
XLA Ops:
  0.7 5.0 %shard_map.118 = (bf16[16,2,320]{2,1,0:T(2,128)(2,1)}, bf16[80,2,256,256]{3,2,1,0:T(8,128)(2,1)}) custom-call(s32[1]{0:T(128)} %bitcast.1.bank_ref, s32[16]{0:T(128)} %indices_ref.5, s32[1]{0:T(128)S(6)} %copy.15.counts_ref, f32[8,64]{1,0:T(8,128)} %constant.18.clone.scalars_ref, f32[2,256]{1,0:T(2,128)} %bitcast.6, f32[1,256]{1,0:T(1,128)} %asd_ref.1, ...), custom_call_target="tpu_custom_call" | custom-call | tf_op jit(solution)/shard_map/pallas_call | solution.py:481
  5.6 17.3 %all_to_all.10 = bf16[16,2,320]{2,1,0:T(2,128)(2,1)S(1)} all-to-all(bf16[16,2,320]{2,1,0:T(2,128)(2,1)} %get-tuple-element.9), channel_id=1, replica_groups={{18,22,26,30,2,6,10,14,16,20,24,28,0,4,8,12},{50,54,58,62,34,38,42,46,4..., dimensions={0} | all-to-all | bytes 40960 | tf_op jit(solution)/shard_map/all_to_all | solution.py:489
  22.9 0.1 broadcast_in_dim.15
  23.0 0.8 %broadcast_in_dim.16 = bf16[16,16,640]{2,1,0:T(8,128)(2,1)} broadcast(bf16[16,640]{1,0:T(8,128)(2,1)S(1)} %broadcast_in_dim.15), dimensions={1,2} | broadcast | bytes 348160 | tf_op jit(solution)/shard_map/broadcast_in_dim | solution.py:490
  23.7 6.7 %all-to-all-start.1 = ((bf16[16,16,640]{2,1,0:T(8,128)(2,1)}), bf16[16,16,640]{2,1,0:T(8,128)(2,1)S(1)}, u32[]{:S(2)}, u32[]{:S(2)}) async-start(bf16[16,16,640]{2,1,0:T(8,128)(2,1)} %broadcast_in_dim.16), calls=%async_computation.1 | async-start | bytes 655360 | tf_op jit(solution)/shard_map/all_to_all | solution.py:491
  30.4 0.0 copy-start
  30.4 0.0 copy-start.1
  30.4 0.0 copy-start.2
  30.4 0.0 copy-start.3
  30.4 6.7 %shard_map.119.waves_ref = bf16[80,2,256,256]{3,2,1,0:T(8,128)(2,1)} custom-call(s32[1]{0:T(128)} %bitcast.1.bank_ref, s32[16]{0:T(128)} %indices_ref.5, s32[1]{0:T(128)S(6)} %copy.15.counts_ref, f32[8,64]{1,0:T(8,128)} %constant.18.clone.scalars_ref, f32[5,256,256]{2,1,0:T(8,128)} %constant.19.clone.powers_hbm, ...), custom_call_target="tpu_custom_call", output_to_operand_aliasing={{}: (5, {})} | custom-call | flops 41943040 | bytes 10485760 | tf_op jit(solution)/shard_map/pallas_call | solution.py:492
  37.1 0.0 copy-start.4
  37.1 0.0 copy-start.5
  37.1 0.0 copy-start.6
  37.2 0.0 all-to-all-done.1.gathered_ref
  37.2 0.0 copy-done
  37.2 0.0 copy-done.1
  37.2 0.0 copy-done.2
  37.2 0.0 copy-done.3
  37.2 7.5 %shard_map.120 = (bf16[2,16,2176]{2,1,0:T(8,128)(2,1)S(1)}, bf16[2,16,2176]{2,1,0:T(8,128)(2,1)S(1)}) custom-call(s32[16]{0:T(128)S(1)} %copy-done.3, s32[1]{0:T(128)S(6)} %copy.15.counts_ref, s32[1]{0:T(128)} %bitcast.half_ref, bf16[16,16,640]{2,1,0:T(8,128)(2,1)S(1)} %all-to-all-done.1.gathered_ref, bf16[2,256,512]{2,1,0:T(8,128)(2,1)S(1)} %copy-done, ...), custom_call_target="tpu_custom_call" | custom-call | tf_op jit(solution)/shard_map/pallas_call | solution.py:505
  44.7 3.9 %all-gather = bf16[4,16,2176]{2,1,0:T(8,128)(2,1)S(1)} all-gather(bf16[2,16,2176]{2,1,0:T(8,128)(2,1)S(1)} %get-tuple-element.12), channel_id=2, replica_groups=mesh['bank'=256,'det'=2] {'det'}, dimensions={0}, use_global_device_ids=true | all-gather | bytes 417792 | tf_op jit(solution)/shard_map/all_gather | solution.py:521
  48.6 0.0 copy-done.4
  48.6 0.0 copy-done.5
  48.6 0.0 copy-done.6
  48.7 3.0 %shard_map.121 = f32[256,2048]{1,0:T(8,128)} custom-call(s32[1]{0:T(128)} %bitcast.half_ref, s32[16]{0:T(128)S(1)} %copy-done.4, f32[16]{0:T(128)S(1)} %copy-done.5, f32[16]{0:T(128)S(1)} %copy-done.6, bf16[2,16,2176]{2,1,0:T(8,128)(2,1)S(1)} %get-tuple-element.11.own_ref, bf16[2,2,16,2176]{3,2,1,0:T(8,128)(2,1)S(1)} %bitcast.5), custom_call_target="tpu_custom_call" | custom-call | tf_op jit(solution)/shard_map/pallas_call | solution.py:522
Async XLA Ops:
  23.7 13.4 %all-to-all-start.1 = ((bf16[16,16,640]{2,1,0:T(8,128)(2,1)}), bf16[16,16,640]{2,1,0:T(8,128)(2,1)S(1)}, u32[]{:S(2)}, u32[]{:S(2)}) async-start(bf16[16,16,640]{2,1,0:T(8,128)(2,1)} %broadcast_in_dim.16), calls=%async_computation.1 | async-start | bytes 655360 | tf_op jit(solution)/shard_map/all_to_all | solution.py:491
  30.4 6.8 %copy-start = (bf16[2,256,512]{2,1,0:T(8,128)(2,1)S(1)}, bf16[2,256,512]{2,1,0:T(8,128)(2,1)}, u32[]{:S(2)}) copy-start(bf16[2,256,512]{2,1,0:T(8,128)(2,1)} %constant.20.clone.first_ref) | copy-start | bytes 1572868
  30.4 6.8 %copy-start.1 = (f32[2,256,256]{2,1,0:T(8,128)S(1)}, f32[2,256,256]{2,1,0:T(8,128)}, u32[]{:S(2)}) copy-start(f32[2,256,256]{2,1,0:T(8,128)} %constant.21.clone.twist_ref) | copy-start | bytes 1572868
  30.4 6.8 %copy-start.2 = (bf16[48,1024]{1,0:T(8,128)(2,1)S(1)}, bf16[48,1024]{1,0:T(8,128)(2,1)}, u32[]{:S(2)}) copy-start(bf16[48,1024]{1,0:T(8,128)(2,1)} %constant.22.clone.last_ref) | copy-start | bytes 294916
  30.4 6.8 %copy-start.3 = (s32[16]{0:T(128)S(1)}, s32[16]{0:T(128)}, u32[]{:S(2)}) copy-start(s32[16]{0:T(128)} %indices_ref.5) | copy-start | bytes 196
  37.1 11.5 %copy-start.4 = (s32[16]{0:T(128)S(1)}, s32[16]{0:T(128)}, u32[]{:S(2)}) copy-start(s32[16]{0:T(128)} %delay_ref.1) | copy-start | bytes 196
  37.1 11.5 %copy-start.5 = (f32[16]{0:T(128)S(1)}, f32[16]{0:T(128)}, u32[]{:S(2)}) copy-start(f32[16]{0:T(128)} %near_gain_ref.1) | copy-start | bytes 196
  37.1 11.5 %copy-start.6 = (f32[16]{0:T(128)S(1)}, f32[16]{0:T(128)}, u32[]{:S(2)}) copy-start(f32[16]{0:T(128)} %far_gain_ref.1) | copy-start | bytes 196

commit v7 on v6

--- a/solution.py
+++ b/solution.py
@@ -29,7 +29,7 @@
 LAST_ROWS = 24
 EARLY = 5
 TILES = HALF // 128
-GROUP = 8
+GROUP = 4
 STAGES = 4
 BIG = 60 * 1024 * 1024
 FILTER_VMEM = 46 * 1024 * 1024
@@ -39,7 +39,7 @@
 SAMPLE_RATE = 2048.0
 
 Z_ORDER = [9, 11, 13, 15, 1, 3, 5, 7, 8, 10, 12, 14, 0, 2, 4, 6]
-XY_ORDER = [(k + 5) % N_XY for k in range(N_XY)]
+XY_ORDER = [(k + 10) % N_XY for k in range(N_XY)]
 
 
 def group_lists():
@@ -405,6 +405,7 @@
     out_ref,
     near,
     pairs,
+    picks,
     tiles,
     sems,
 ):
@@ -432,11 +433,12 @@
 
     for group in range(0, TILES, GROUP):
         for sky in range(0, SKY, 2):
-            shift = jnp.where(col_id < 128, delay_ref[sky] + 64, delay_ref[sky + 1] - 64)
-            pick = jnp.where(row_id == col_id + shift, 1.0, 0.0).astype(jnp.bfloat16)
+            if group == 0:
+                shift = jnp.where(col_id < 128, delay_ref[sky] + 64, delay_ref[sky + 1] - 64)
+                picks[sky // 2] = jnp.where(row_id == col_id + shift, 1.0, 0.0).astype(jnp.bfloat16)
             delayed = jnp.dot(
                 pairs[32 * group : 32 * (group + GROUP), :],
-                pick,
+                picks[sky // 2],
                 preferred_element_type=jnp.float32,
             )
             for side in range(2):
@@ -527,6 +529,7 @@
         scratch_shapes=[
             pltpu.VMEM((2 * TPL_DEV * TILES, 128), jnp.float32),
             pltpu.VMEM((2 * TPL_DEV * TILES, 256), jnp.bfloat16),
+            pltpu.VMEM((SKY // 2, 256, 256), jnp.bfloat16),
             pltpu.VMEM((TILES, TPL_DEV * SKY, 128), jnp.float32),
             pltpu.SemaphoreType.DMA((TILES,)),
         ],

time: 52 us -> 51.7 us (level)
  the two profiles are of different devices: /device:TPU:31 before, /device:TPU:65 now
where the time goes in v7:
time: 51.7 us; the launch traced here: 51.4 us
  Pallas kernels  21.9 us (42%)
  blocking collectives  19.1 us (37%)
  starting transfers between devices  8.74 us (17%)
  local copies, waits for them, and re-layouts  0.89 us (2%)
  between operations  0.77 us (1%)
    all_to_all x1, blocking collectives, on_device(): line = lax.all_to_all(payload, 'bank', 0, 0, axis_index_groups=z_groups)  15.4 us
    all_to_all x1, starting transfers between devices, on_device(): plane = lax.all_to_all(spread, 'bank', 0, 0, axis_index_groups=xy_groups)  8.74 us
    pallas_call x1, Pallas kernels, on_device(): pl.pallas_call(filter_kernel, out_shape=(window, window), in_specs=[SMEM]...  7.52 us
    pallas_call x1, Pallas kernels, on_device(): pl.pallas_call(wave_kernel, out_shape=room, in_specs=[SMEM] * 4 + [ANY] *...  6.68 us
    pallas_call x1, Pallas kernels, on_device(): pl.pallas_call(prepare_kernel, out_shape=(jax.ShapeDtypeStruct((N_Z, 2, P...  4.96 us
    all_gather x1, blocking collectives, on_device(): got = lax.all_gather(send, 'det', axis=0)  3.67 us
    pallas_call x1, Pallas kernels, on_device(): pl.pallas_call(coherent_kernel, out_shape=jax.ShapeDtypeStruct((TPL_DEV *...  2.73 us
  transfers between devices with their start and end apart: 1, of which 0 were waited for; matrix products, arithmetic and copies ran while one was open for 0% of the time, Pallas kernels for 13%

profile of v7, /device:TPU:65, one launch (start us, length us, event | category | flops | bytes accessed | tf_op | source)
XLA Modules:
  0.0 51.4 jit_solution(7585605458015020033)
XLA Ops:
  0.7 5.0 %shard_map.118 = (bf16[16,2,320]{2,1,0:T(2,128)(2,1)}, bf16[80,2,256,256]{3,2,1,0:T(8,128)(2,1)}) custom-call(s32[1]{0:T(128)} %bitcast.1.bank_ref, s32[16]{0:T(128)} %indices_ref.5, s32[1]{0:T(128)S(6)} %copy.15.counts_ref, f32[8,64]{1,0:T(8,128)} %constant.18.clone.scalars_ref, f32[2,256]{1,0:T(2,128)} %bitcast.6, f32[1,256]{1,0:T(1,128)} %asd_ref.1, ...), custom_call_target="tpu_custom_call" | custom-call | tf_op jit(solution)/shard_map/pallas_call | solution.py:483
  5.6 15.4 %all_to_all.10 = bf16[16,2,320]{2,1,0:T(2,128)(2,1)S(1)} all-to-all(bf16[16,2,320]{2,1,0:T(2,128)(2,1)} %get-tuple-element.9), channel_id=1, replica_groups={{18,22,26,30,2,6,10,14,16,20,24,28,0,4,8,12},{50,54,58,62,34,38,42,46,4..., dimensions={0} | all-to-all | bytes 40960 | tf_op jit(solution)/shard_map/all_to_all | solution.py:491
  21.0 0.1 broadcast_in_dim.15
  21.1 0.8 %broadcast_in_dim.16 = bf16[16,16,640]{2,1,0:T(8,128)(2,1)} broadcast(bf16[16,640]{1,0:T(8,128)(2,1)S(1)} %broadcast_in_dim.15), dimensions={1,2} | broadcast | bytes 348160 | tf_op jit(solution)/shard_map/broadcast_in_dim | solution.py:492
  21.9 8.7 %all-to-all-start.1 = ((bf16[16,16,640]{2,1,0:T(8,128)(2,1)}), bf16[16,16,640]{2,1,0:T(8,128)(2,1)S(1)}, u32[]{:S(2)}, u32[]{:S(2)}) async-start(bf16[16,16,640]{2,1,0:T(8,128)(2,1)} %broadcast_in_dim.16), calls=%async_computation.1 | async-start | bytes 655360 | tf_op jit(solution)/shard_map/all_to_all | solution.py:493
  30.6 0.0 copy-start
  30.6 0.0 copy-start.1
  30.6 0.0 copy-start.2
  30.6 0.0 copy-start.3
  30.7 6.7 %shard_map.119.waves_ref = bf16[80,2,256,256]{3,2,1,0:T(8,128)(2,1)} custom-call(s32[1]{0:T(128)} %bitcast.1.bank_ref, s32[16]{0:T(128)} %indices_ref.5, s32[1]{0:T(128)S(6)} %copy.15.counts_ref, f32[8,64]{1,0:T(8,128)} %constant.18.clone.scalars_ref, f32[5,256,256]{2,1,0:T(8,128)} %constant.19.clone.powers_hbm, ...), custom_call_target="tpu_custom_call", output_to_operand_aliasing={{}: (5, {})} | custom-call | flops 41943040 | bytes 10485760 | tf_op jit(solution)/shard_map/pallas_call | solution.py:494
  37.3 0.0 copy-start.4
  37.4 0.0 copy-start.5
  37.4 0.0 copy-start.6
  37.4 0.0 all-to-all-done.1.gathered_ref
  37.4 0.0 copy-done
  37.4 0.0 copy-done.1
  37.4 0.0 copy-done.2
  37.4 0.0 copy-done.3
  37.4 7.5 %shard_map.120 = (bf16[2,16,2176]{2,1,0:T(8,128)(2,1)S(1)}, bf16[2,16,2176]{2,1,0:T(8,128)(2,1)S(1)}) custom-call(s32[16]{0:T(128)S(1)} %copy-done.3, s32[1]{0:T(128)S(6)} %copy.15.counts_ref, s32[1]{0:T(128)} %bitcast.half_ref, bf16[16,16,640]{2,1,0:T(8,128)(2,1)S(1)} %all-to-all-done.1.gathered_ref, bf16[2,256,512]{2,1,0:T(8,128)(2,1)S(1)} %copy-done, ...), custom_call_target="tpu_custom_call" | custom-call | tf_op jit(solution)/shard_map/pallas_call | solution.py:507
  45.0 3.7 %all-gather = bf16[4,16,2176]{2,1,0:T(8,128)(2,1)S(1)} all-gather(bf16[2,16,2176]{2,1,0:T(8,128)(2,1)S(1)} %get-tuple-element.12), channel_id=2, replica_groups=mesh['bank'=256,'det'=2] {'det'}, dimensions={0}, use_global_device_ids=true | all-gather | bytes 417792 | tf_op jit(solution)/shard_map/all_gather | solution.py:523
  48.6 0.0 copy-done.4
  48.6 0.0 copy-done.5
  48.6 0.0 copy-done.6
  48.6 2.7 %shard_map.121 = f32[256,2048]{1,0:T(8,128)} custom-call(s32[1]{0:T(128)} %bitcast.half_ref, s32[16]{0:T(128)S(1)} %copy-done.4, f32[16]{0:T(128)S(1)} %copy-done.5, f32[16]{0:T(128)S(1)} %copy-done.6, bf16[2,16,2176]{2,1,0:T(8,128)(2,1)S(1)} %get-tuple-element.11.own_ref, bf16[2,2,16,2176]{3,2,1,0:T(8,128)(2,1)S(1)} %bitcast.5), custom_call_target="tpu_custom_call" | custom-call | tf_op jit(solution)/shard_map/pallas_call | solution.py:524
Async XLA Ops:
  21.9 15.5 %all-to-all-start.1 = ((bf16[16,16,640]{2,1,0:T(8,128)(2,1)}), bf16[16,16,640]{2,1,0:T(8,128)(2,1)S(1)}, u32[]{:S(2)}, u32[]{:S(2)}) async-start(bf16[16,16,640]{2,1,0:T(8,128)(2,1)} %broadcast_in_dim.16), calls=%async_computation.1 | async-start | bytes 655360 | tf_op jit(solution)/shard_map/all_to_all | solution.py:493
  30.6 6.8 %copy-start = (bf16[2,256,512]{2,1,0:T(8,128)(2,1)S(1)}, bf16[2,256,512]{2,1,0:T(8,128)(2,1)}, u32[]{:S(2)}) copy-start(bf16[2,256,512]{2,1,0:T(8,128)(2,1)} %constant.20.clone.first_ref) | copy-start | bytes 1572868
  30.6 6.8 %copy-start.1 = (f32[2,256,256]{2,1,0:T(8,128)S(1)}, f32[2,256,256]{2,1,0:T(8,128)}, u32[]{:S(2)}) copy-start(f32[2,256,256]{2,1,0:T(8,128)} %constant.21.clone.twist_ref) | copy-start | bytes 1572868
  30.6 6.8 %copy-start.2 = (bf16[48,1024]{1,0:T(8,128)(2,1)S(1)}, bf16[48,1024]{1,0:T(8,128)(2,1)}, u32[]{:S(2)}) copy-start(bf16[48,1024]{1,0:T(8,128)(2,1)} %constant.22.clone.last_ref) | copy-start | bytes 294916
  30.6 6.8 %copy-start.3 = (s32[16]{0:T(128)S(1)}, s32[16]{0:T(128)}, u32[]{:S(2)}) copy-start(s32[16]{0:T(128)} %indices_ref.5) | copy-start | bytes 196
  37.3 11.3 %copy-start.4 = (s32[16]{0:T(128)S(1)}, s32[16]{0:T(128)}, u32[]{:S(2)}) copy-start(s32[16]{0:T(128)} %delay_ref.1) | copy-start | bytes 196
  37.4 11.3 %copy-start.5 = (f32[16]{0:T(128)S(1)}, f32[16]{0:T(128)}, u32[]{:S(2)}) copy-start(f32[16]{0:T(128)} %near_gain_ref.1) | copy-start | bytes 196
  37.4 11.3 %copy-start.6 = (f32[16]{0:T(128)S(1)}, f32[16]{0:T(128)}, u32[]{:S(2)}) copy-start(f32[16]{0:T(128)} %far_gain_ref.1) | copy-start | bytes 196

commit v8 on v7

--- a/solution.py
+++ b/solution.py
@@ -39,7 +39,7 @@
 SAMPLE_RATE = 2048.0
 
 Z_ORDER = [9, 11, 13, 15, 1, 3, 5, 7, 8, 10, 12, 14, 0, 2, 4, 6]
-XY_ORDER = [(k + 10) % N_XY for k in range(N_XY)]
+XY_ORDER = [(k + 5) % N_XY for k in range(N_XY)]
 
 
 def group_lists():

time: 51.7 us -> 52.6 us (1.017)
  the two profiles are of different devices: /device:TPU:65 before, /device:TPU:9 now
where the time goes in v8:
time: 52.6 us; the launch traced here: 52.2 us
  Pallas kernels  21.9 us (42%)
  blocking collectives  21.6 us (41%)
  starting transfers between devices  6.08 us (12%)
  waiting for transfers between devices  0.98 us (2%)
  local copies, waits for them, and re-layouts  0.89 us (2%)
  between operations  0.75 us (1%)
    all_to_all x1, blocking collectives, on_device(): line = lax.all_to_all(payload, 'bank', 0, 0, axis_index_groups=z_groups)  17.3 us
    pallas_call x1, Pallas kernels, on_device(): pl.pallas_call(filter_kernel, out_shape=(window, window), in_specs=[SMEM]...  7.51 us
    pallas_call x1, Pallas kernels, on_device(): pl.pallas_call(wave_kernel, out_shape=room, in_specs=[SMEM] * 4 + [ANY] *...  6.68 us
    all_to_all x1, starting transfers between devices, on_device(): plane = lax.all_to_all(spread, 'bank', 0, 0, axis_index_groups=xy_groups)  6.08 us
    pallas_call x1, Pallas kernels, on_device(): pl.pallas_call(prepare_kernel, out_shape=(jax.ShapeDtypeStruct((N_Z, 2, P...  4.96 us
    all_gather x1, blocking collectives, on_device(): got = lax.all_gather(send, 'det', axis=0)  4.35 us
    pallas_call x1, Pallas kernels, on_device(): pl.pallas_call(coherent_kernel, out_shape=jax.ShapeDtypeStruct((TPL_DEV *...  2.73 us
  transfers between devices with their start and end apart: 1, of which 1 were waited for; matrix products, arithmetic and copies ran while one was open for 0% of the time, Pallas kernels for 13%

profile of v8, /device:TPU:9, one launch (start us, length us, event | category | flops | bytes accessed | tf_op | source)
XLA Modules:
  0.0 52.2 jit_solution(10517584095049131015)
XLA Ops:
  0.7 5.0 %shard_map.118 = (bf16[16,2,320]{2,1,0:T(2,128)(2,1)}, bf16[80,2,256,256]{3,2,1,0:T(8,128)(2,1)}) custom-call(s32[1]{0:T(128)} %bitcast.1.bank_ref, s32[16]{0:T(128)} %indices_ref.5, s32[1]{0:T(128)S(6)} %copy.15.counts_ref, f32[8,64]{1,0:T(8,128)} %constant.18.clone.scalars_ref, f32[2,256]{1,0:T(2,128)} %bitcast.6, f32[1,256]{1,0:T(1,128)} %asd_ref.1, ...), custom_call_target="tpu_custom_call" | custom-call | tf_op jit(solution)/shard_map/pallas_call | solution.py:483
  5.6 17.3 %all_to_all.10 = bf16[16,2,320]{2,1,0:T(2,128)(2,1)S(1)} all-to-all(bf16[16,2,320]{2,1,0:T(2,128)(2,1)} %get-tuple-element.9), channel_id=1, replica_groups={{18,22,26,30,2,6,10,14,16,20,24,28,0,4,8,12},{50,54,58,62,34,38,42,46,4..., dimensions={0} | all-to-all | bytes 40960 | tf_op jit(solution)/shard_map/all_to_all | solution.py:491
  22.9 0.1 broadcast_in_dim.15
  23.0 0.8 %broadcast_in_dim.16 = bf16[16,16,640]{2,1,0:T(8,128)(2,1)} broadcast(bf16[16,640]{1,0:T(8,128)(2,1)S(1)} %broadcast_in_dim.15), dimensions={1,2} | broadcast | bytes 348160 | tf_op jit(solution)/shard_map/broadcast_in_dim | solution.py:492
  23.7 6.1 %all-to-all-start.1 = ((bf16[16,16,640]{2,1,0:T(8,128)(2,1)}), bf16[16,16,640]{2,1,0:T(8,128)(2,1)S(1)}, u32[]{:S(2)}, u32[]{:S(2)}) async-start(bf16[16,16,640]{2,1,0:T(8,128)(2,1)} %broadcast_in_dim.16), calls=%async_computation.1 | async-start | bytes 655360 | tf_op jit(solution)/shard_map/all_to_all | solution.py:493
  29.8 0.0 copy-start
  29.8 0.0 copy-start.1
  29.8 0.0 copy-start.2
  29.8 0.0 copy-start.3
  29.9 6.7 %shard_map.119.waves_ref = bf16[80,2,256,256]{3,2,1,0:T(8,128)(2,1)} custom-call(s32[1]{0:T(128)} %bitcast.1.bank_ref, s32[16]{0:T(128)} %indices_ref.5, s32[1]{0:T(128)S(6)} %copy.15.counts_ref, f32[8,64]{1,0:T(8,128)} %constant.18.clone.scalars_ref, f32[5,256,256]{2,1,0:T(8,128)} %constant.19.clone.powers_hbm, ...), custom_call_target="tpu_custom_call", output_to_operand_aliasing={{}: (5, {})} | custom-call | flops 41943040 | bytes 10485760 | tf_op jit(solution)/shard_map/pallas_call | solution.py:494
  36.5 0.0 copy-start.4
  36.6 0.0 copy-start.5
  36.6 0.0 copy-start.6
  36.6 1.0 %all-to-all-done.1.gathered_ref = bf16[16,16,640]{2,1,0:T(8,128)(2,1)S(1)} async-done(((bf16[16,16,640]{2,1,0:T(8,128)(2,1)}), bf16[16,16,640]{2,1,0:T(8,128)(2,1)S(1)}, u32[]{:S(2)}, u32[]{:S(2)}) %all-to-all-start.1) | async-done | bytes 327712 | tf_op jit(solution)/shard_map/all_to_all | solution.py:493
  37.6 0.0 copy-done
  37.6 0.0 copy-done.1
  37.6 0.0 copy-done.2
  37.6 0.0 copy-done.3
  37.6 7.5 %shard_map.120 = (bf16[2,16,2176]{2,1,0:T(8,128)(2,1)S(1)}, bf16[2,16,2176]{2,1,0:T(8,128)(2,1)S(1)}) custom-call(s32[16]{0:T(128)S(1)} %copy-done.3, s32[1]{0:T(128)S(6)} %copy.15.counts_ref, s32[1]{0:T(128)} %bitcast.half_ref, bf16[16,16,640]{2,1,0:T(8,128)(2,1)S(1)} %all-to-all-done.1.gathered_ref, bf16[2,256,512]{2,1,0:T(8,128)(2,1)S(1)} %copy-done, ...), custom_call_target="tpu_custom_call" | custom-call | tf_op jit(solution)/shard_map/pallas_call | solution.py:507
  45.1 4.3 %all-gather = bf16[4,16,2176]{2,1,0:T(8,128)(2,1)S(1)} all-gather(bf16[2,16,2176]{2,1,0:T(8,128)(2,1)S(1)} %get-tuple-element.12), channel_id=2, replica_groups=mesh['bank'=256,'det'=2] {'det'}, dimensions={0}, use_global_device_ids=true | all-gather | bytes 417792 | tf_op jit(solution)/shard_map/all_gather | solution.py:523
  49.4 0.0 copy-done.4
  49.4 0.0 copy-done.5
  49.4 0.0 copy-done.6
  49.5 2.7 %shard_map.121 = f32[256,2048]{1,0:T(8,128)} custom-call(s32[1]{0:T(128)} %bitcast.half_ref, s32[16]{0:T(128)S(1)} %copy-done.4, f32[16]{0:T(128)S(1)} %copy-done.5, f32[16]{0:T(128)S(1)} %copy-done.6, bf16[2,16,2176]{2,1,0:T(8,128)(2,1)S(1)} %get-tuple-element.11.own_ref, bf16[2,2,16,2176]{3,2,1,0:T(8,128)(2,1)S(1)} %bitcast.5), custom_call_target="tpu_custom_call" | custom-call | tf_op jit(solution)/shard_map/pallas_call | solution.py:524
Async XLA Ops:
  23.7 13.8 %all-to-all-start.1 = ((bf16[16,16,640]{2,1,0:T(8,128)(2,1)}), bf16[16,16,640]{2,1,0:T(8,128)(2,1)S(1)}, u32[]{:S(2)}, u32[]{:S(2)}) async-start(bf16[16,16,640]{2,1,0:T(8,128)(2,1)} %broadcast_in_dim.16), calls=%async_computation.1 | async-start | bytes 655360 | tf_op jit(solution)/shard_map/all_to_all | solution.py:493
  29.8 7.7 %copy-start = (bf16[2,256,512]{2,1,0:T(8,128)(2,1)S(1)}, bf16[2,256,512]{2,1,0:T(8,128)(2,1)}, u32[]{:S(2)}) copy-start(bf16[2,256,512]{2,1,0:T(8,128)(2,1)} %constant.20.clone.first_ref) | copy-start | bytes 1572868
  29.8 7.7 %copy-start.1 = (f32[2,256,256]{2,1,0:T(8,128)S(1)}, f32[2,256,256]{2,1,0:T(8,128)}, u32[]{:S(2)}) copy-start(f32[2,256,256]{2,1,0:T(8,128)} %constant.21.clone.twist_ref) | copy-start | bytes 1572868
  29.8 7.7 %copy-start.2 = (bf16[48,1024]{1,0:T(8,128)(2,1)S(1)}, bf16[48,1024]{1,0:T(8,128)(2,1)}, u32[]{:S(2)}) copy-start(bf16[48,1024]{1,0:T(8,128)(2,1)} %constant.22.clone.last_ref) | copy-start | bytes 294916
  29.8 7.7 %copy-start.3 = (s32[16]{0:T(128)S(1)}, s32[16]{0:T(128)}, u32[]{:S(2)}) copy-start(s32[16]{0:T(128)} %indices_ref.5) | copy-start | bytes 196
  36.5 12.9 %copy-start.4 = (s32[16]{0:T(128)S(1)}, s32[16]{0:T(128)}, u32[]{:S(2)}) copy-start(s32[16]{0:T(128)} %delay_ref.1) | copy-start | bytes 196
  36.6 12.9 %copy-start.5 = (f32[16]{0:T(128)S(1)}, f32[16]{0:T(128)}, u32[]{:S(2)}) copy-start(f32[16]{0:T(128)} %near_gain_ref.1) | copy-start | bytes 196
  36.6 12.9 %copy-start.6 = (f32[16]{0:T(128)S(1)}, f32[16]{0:T(128)}, u32[]{:S(2)}) copy-start(f32[16]{0:T(128)} %far_gain_ref.1) | copy-start | bytes 196
